TPU v7x, 128 devices: a whole 4x4x4 slice. The times are simulated.
128 devices in a mesh: px: 8 (over x, core), py: 16 (over z, y).
Axes of the slice: x: 4, y: 4, z: 4, core: 2. Of those that a mesh axis runs over, the one named last changes fastest.
Arguments:
- conserved: float32 [5, 6, 6, 6, 16384], P(None, None, None, None, ('px', 'py')), may hold values from -1 to 5, as said below
- flow_lists: int32 [128, 2, 32], P(('px', 'py')), may hold values from 0 to 127, as said below
- span_lists: int32 [128, 2, 64], P(('px', 'py')), may hold values from 0 to 127, as said below
- face_source: int32 [6, 16384], P(None, ('px', 'py')), may hold values from 0 to 1727, as said below
Outputs:
- advanced: float32 [5, 6, 6, 6, 16384], P(None, None, None, None, ('px', 'py'))
- register: float32 [5, 6, 6, 6, 16384], P(None, None, None, None, ('px', 'py'))
Inputs may be any that keep to these rules, and one draw needn't show every extreme that they name: `conserved`: density lies in 0.7 to 1.3, each velocity component within 0.75 in magnitude, pressure in 0.55 to 1.45. Entry k of flow_lists[d, 0] (of flow_lists[d, 1]) is the slot of the element whose side 0 (side 1) carries the k-th face of the block boundary toward the block one lower (one higher) along the flow, cyclically; the receiving block lists its matching faces in the same order. Every block boundary along the flow has 32 faces. Entry k of span_lists[d, 0] (of span_lists[d, 1]) is the slot of the element whose side 4 (side 5) carries the k-th face of the block boundary toward the block one lower (one higher) along the span, cyclically, in the order shared with that block; a block boundary has at most 64 faces, some boundary has exactly 64, and entries past a boundary's faces hold 0. `face_source`: Sides 2 and 3 at the channel walls point at the wall values; slots outside a device's live block point at wall values on all six sides; every other side points at the side of the element that shares its face, which points back.
All inputs are finite; a program needn't handle non-finite values.
Results may differ from a plain program's by a relative error of at most 0.0003.
Values sent between devices are 32-bit elements; how exact they have to be, the bound alone decides.
No kernel may reach another device: no remote copies, remote signals or barrier semaphores. Data moves between devices by JAX's collectives and lax.ppermute only.
A program may use at most 192 MiB of HBM per device.

v0:
```python
import math

import jax
import jax.numpy as jnp
import numpy as np
from jax import lax
from jax.experimental import pallas as pl
from jax.experimental.pallas import tpu as pltpu
from jax.sharding import PartitionSpec as P

GAMMA = 1.4
VISCOSITY = 0.02
TIME_STEP = 0.01
RK_A = (
    0.0,
    -567301805773.0 / 1357537059087.0,
    -2404267990393.0 / 2016746695238.0,
    -3550918686646.0 / 2091501179385.0,
    -1275806237668.0 / 842570457699.0,
)
RK_B = (
    1432997174477.0 / 9575080441755.0,
    5161836677717.0 / 13612068292357.0,
    1720146321549.0 / 2090206949498.0,
    3134564353537.0 / 4481467310338.0,
    2277821191437.0 / 14882151754819.0,
)


def lobatto_tables():
    inner_node = math.sqrt(1.0 / 3.0 - 2.0 * math.sqrt(7.0) / 21.0)
    outer_node = math.sqrt(1.0 / 3.0 + 2.0 * math.sqrt(7.0) / 21.0)
    points = np.array([-1.0, -outer_node, -inner_node, inner_node, outer_node, 1.0])
    legendre = (63.0 * points**5 - 70.0 * points**3 + 15.0 * points) / 8.0
    weights = 2.0 / (30.0 * legendre * legendre)
    identity = np.eye(6)
    differences = points[:, None] - points[None, :] + identity
    barycentric = 1.0 / np.prod(differences, axis=1)
    matrix = barycentric[None, :] / barycentric[:, None] / differences
    matrix = matrix * (1.0 - identity)
    matrix = matrix - identity * np.sum(matrix, axis=1)[:, None]
    return matrix, weights


DM, WEIGHTS = lobatto_tables()
DM2 = DM @ DM
LIFT = 1.0 / WEIGHTS[0]
NV = 5
VROWS = 320
FIELD = (NV * VROWS, 128)
FACE0 = (2, 60, 8, 128)
FACE2 = (2, 50, 8, 128)
FLOW_PACK = (15, 8, 128)
SPAN_PACK = (25, 8, 128)
CODES = (10, 8, 128)
RECEIVED = 256
WALL = 512


def tile_at(ref, row):
    return ref[pl.ds(pl.multiple_of(row, 8), 8), :]


def put_tile(ref, row, value):
    ref[pl.ds(pl.multiple_of(row, 8), 8), :] = value


def line_at(ref, var, chunk, k):
    return ref[pl.ds(var * VROWS + chunk * 64 + k, 8, stride=8), :]


def put_line(ref, var, chunk, k, value):
    ref[pl.ds(var * VROWS + chunk * 64 + k, 8, stride=8), :] = value


def take_lanes(value, index):
    return jnp.take_along_axis(value, index, axis=1, mode="promise_in_bounds")


def even_odd(values):
    even = [values[m] + values[5 - m] for m in range(3)]
    odd = [values[m] - values[5 - m] for m in range(3)]
    return even, odd


def combine(coefficients, terms):
    total = None
    for coefficient, term in zip(coefficients, terms):
        part = float(coefficient) * term
        total = part if total is None else total + part
    return total


def end_derivatives(values):
    even, odd = even_odd(values)
    first = combine([(DM[0, m] + DM[0, 5 - m]) / 2 for m in range(3)], even)
    second = combine([(DM[0, m] - DM[0, 5 - m]) / 2 for m in range(3)], odd)
    return first + second, second - first


def second_derivative(values, scale):
    even, odd = even_odd(values)
    result = [None] * 6
    for i in range(3):
        first = combine([scale * (DM2[i, m] + DM2[i, 5 - m]) / 2 for m in range(3)], even)
        second = combine([scale * (DM2[i, m] - DM2[i, 5 - m]) / 2 for m in range(3)], odd)
        result[i] = first + second
        result[5 - i] = first - second
    return result


def half_primitive(state):
    inverse = 1.0 / state[0]
    half = 0.5 * inverse
    velocity = [half * state[1], half * state[2], half * state[3]]
    kinetic = velocity[0] * state[1] + velocity[1] * state[2] + velocity[2] * state[3]
    pressure = (0.5 * (GAMMA - 1.0)) * (state[4] - kinetic)
    return [0.5 * state[0], velocity[0], velocity[1], velocity[2], pressure, half * state[4]]


def line_fluxes(nodes, direction):
    sums = [[None] * NV for _ in range(6)]

    def add(node, var, value, sign):
        old = sums[node][var]
        if old is None:
            sums[node][var] = value if sign > 0 else -value
        else:
            sums[node][var] = old + value if sign > 0 else old - value

    for i in range(6):
        for m in range(i + 1, 6):
            weight = float(2.0 * WEIGHTS[i] * DM[i, m])
            left, right = nodes[i], nodes[m]
            density, v0, v1, v2, pressure, specific = [left[n] + right[n] for n in range(6)]
            velocity = (v0, v1, v2)
            mass = (weight * density) * velocity[direction]
            scaled = weight * pressure
            flux = [mass, mass * v0, mass * v1, mass * v2, mass * specific + scaled * velocity[direction]]
            flux[1 + direction] = flux[1 + direction] + scaled
            for var in range(NV):
                add(i, var, flux[var], 1)
                add(m, var, flux[var], -1)
    return sums


def rusanov(left, right, direction):
    def parts(state):
        inverse = 1.0 / state[0]
        velocity = state[1 + direction] * inverse
        kinetic = state[1] * state[1] + state[2] * state[2] + state[3] * state[3]
        pressure = (GAMMA - 1.0) * (state[4] - 0.5 * inverse * kinetic)
        speed = jnp.abs(velocity) + jnp.sqrt(GAMMA * pressure * inverse)
        flux = [state[1 + direction], state[1] * velocity, state[2] * velocity, state[3] * velocity]
        flux.append((state[4] + pressure) * velocity)
        flux[1 + direction] = flux[1 + direction] + pressure
        return flux, speed

    left_flux, left_speed = parts(left)
    right_flux, right_speed = parts(right)
    speed = jnp.maximum(left_speed, right_speed)
    return [
        0.5 * ((left_flux[n] + right_flux[n]) - speed * (right[n] - left[n])) for n in range(NV)
    ]


def face_terms(low, high, direction):
    low_flux = rusanov(low[2], low[0], direction)
    high_flux = rusanov(high[0], high[2], direction)
    visc = 0.5 * VISCOSITY * LIFT
    end_low, end_high, jump_low, jump_high = [], [], [], []
    for n in range(NV):
        end_low.append(LIFT * low_flux[n] - visc * (low[3][n] - low[1][n]))
        end_high.append(visc * (high[3][n] - high[1][n]) - LIFT * high_flux[n])
        jump_low.append(visc * (low[2][n] - low[0][n]))
        jump_high.append(visc * (high[2][n] - high[0][n]))
    return end_low, end_high, jump_low, jump_high


def add_faces(values, terms, var, scale):
    end_low, end_high, jump_low, jump_high = terms
    result = []
    for i in range(6):
        value = values[i] + float(scale * DM[i, 5]) * jump_high[var] - float(scale * DM[i, 0]) * jump_low[var]
        if i == 0:
            value = value + scale * end_low[var]
        if i == 5:
            value = value + scale * end_high[var]
        result.append(value)
    return result


def make_faces(field, face0, face2):
    def flow_row(j, carry):
        for v in range(NV):
            values = [tile_at(field, v * VROWS + i * 48 + j * 8) for i in range(6)]
            first, last = end_derivatives(values)
            face0[0, v * 6 + j] = values[0]
            face0[1, v * 6 + j] = values[5]
            face0[0, (NV + v) * 6 + j] = first
            face0[1, (NV + v) * 6 + j] = last
        return carry

    lax.fori_loop(0, 6, flow_row, 0)

    def span_row(chunk, carry):
        for v in range(NV):
            values = [line_at(field, v, chunk, k) for k in range(6)]
            first, last = end_derivatives(values)
            face2[0, v * 5 + chunk] = values[0]
            face2[1, v * 5 + chunk] = values[5]
            face2[0, (NV + v) * 5 + chunk] = first
            face2[1, (NV + v) * 5 + chunk] = last
        return carry

    lax.fori_loop(0, 5, span_row, 0)


def pack_faces(parity, codes, face0, face2, flow_a, flow_b, span_a, span_b):
    lane = lax.broadcasted_iota(jnp.int32, (8, 128), 1)
    flow_odd, span_odd = parity[0], parity[1]
    for side, out in ((1 - flow_odd, flow_a), (flow_odd, flow_b)):
        index = codes[6 + side]
        for t in range(15):
            packed = take_lanes(face0[side, t], index)
            for g in range(1, 4):
                packed = jnp.where(lane >= 32 * g, take_lanes(face0[side, 15 * g + t], index), packed)
            out[t] = packed
    for side, out in ((1 - span_odd, span_a), (span_odd, span_b)):
        index = codes[8 + side]
        for t in range(25):
            out[t] = jnp.where(
                lane >= 64, take_lanes(face2[side, 25 + t], index), take_lanes(face2[side, t], index)
            )


def first_kernel(
    parity, conserved, lists, field, codes, face0, face2, flow_a, flow_b, span_a, span_b
):
    for v in range(NV):
        for i in range(6):
            for j in range(6):
                field[pl.ds(v * VROWS + i * 48 + j * 8, 6), :] = conserved[v, i, j]
    for side in range(6):
        column = lists[pl.ds(side, 1), :]
        mask = 31 if side < 2 else 63
        offset = 768 if side < 2 else 832
        code = jnp.where(
            column < 768,
            column & 127,
            jnp.where(column < 960, ((column - offset) & mask) + RECEIVED, WALL),
        )
        codes[side] = jnp.broadcast_to(code, (8, 128))
    for row in range(6, 10):
        codes[row] = jnp.broadcast_to(lists[pl.ds(row, 1), :], (8, 128))
    make_faces(field, face0, face2)
    pack_faces(parity, codes, face0, face2, flow_a, flow_b, span_a, span_b)


def volume_kernel(section, field, register, codes, face0, face2, base, near0, near2, prims):
    step = TIME_STEP

    def primitives(n, carry):
        for u in range(4):
            row = (n * 4 + u) * 8
            values = half_primitive([tile_at(field, v * VROWS + row) for v in range(NV)])
            for q in range(6):
                put_tile(prims, q * VROWS + row, values[q])
        return carry

    lax.fori_loop(0, 9, primitives, 0)

    def viscous_and_flux(lines, nodes, direction, var, sums):
        second = second_derivative(lines[var], step * VISCOSITY)
        return [second[i] - float(step / WEIGHTS[i]) * sums[i][var] for i in range(6)]

    def flow_row(j, carry):
        row = j * 8
        nodes = [[tile_at(prims, q * VROWS + i * 48 + row) for q in range(6)] for i in range(6)]
        sums = line_fluxes(nodes, 0)
        for v in range(NV):
            line = [tile_at(field, v * VROWS + i * 48 + row) for i in range(6)]
            second = second_derivative(line, step * VISCOSITY)
            for i in range(6):
                value = second[i] - float(step / WEIGHTS[i]) * sums[i][v]
                if section > 0:
                    value = value + RK_A[section] * tile_at(register, v * VROWS + i * 48 + row)
                put_tile(base, v * VROWS + i * 48 + row, value)
        return carry

    lax.fori_loop(0, 6, flow_row, 0)

    low_code, high_code = codes[2], codes[3]
    low_index, high_index = low_code & 127, high_code & 127
    low_wall, high_wall = low_code >= WALL, high_code >= WALL

    def wall_row(i, carry):
        row = i * 48
        nodes = [[tile_at(prims, q * VROWS + row + j * 8) for q in range(6)] for j in range(6)]
        sums = line_fluxes(nodes, 1)
        lines = [[tile_at(field, v * VROWS + row + j * 8) for j in range(6)] for v in range(NV)]
        ends = [end_derivatives(line) for line in lines]
        low = ([line[0] for line in lines], [end[0] for end in ends], [], [])
        high = ([line[5] for line in lines], [end[1] for end in ends], [], [])
        for v in range(NV):
            sign = -1.0 if 1 <= v <= 3 else 1.0
            low[2].append(jnp.where(low_wall, sign * low[0][v], take_lanes(high[0][v], low_index)))
            low[3].append(jnp.where(low_wall, low[1][v], take_lanes(high[1][v], low_index)))
            high[2].append(jnp.where(high_wall, sign * high[0][v], take_lanes(low[0][v], high_index)))
            high[3].append(jnp.where(high_wall, high[1][v], take_lanes(low[1][v], high_index)))
        terms = face_terms(low, high, 1)
        for v in range(NV):
            second = second_derivative(lines[v], step * VISCOSITY)
            values = [second[j] - float(step / WEIGHTS[j]) * sums[j][v] for j in range(6)]
            values = add_faces(values, terms, v, step)
            for j in range(6):
                where = v * VROWS + row + j * 8
                put_tile(base, where, tile_at(base, where) + values[j])
        return carry

    lax.fori_loop(0, 6, wall_row, 0)

    def span_row(chunk, carry):
        nodes = [[line_at(prims, q, chunk, k) for q in range(6)] for k in range(6)]
        sums = line_fluxes(nodes, 2)
        for v in range(NV):
            line = [line_at(field, v, chunk, k) for k in range(6)]
            second = second_derivative(line, step * VISCOSITY)
            for k in range(6):
                value = second[k] - float(step / WEIGHTS[k]) * sums[k][v]
                put_line(base, v, chunk, k, line_at(base, v, chunk, k) + value)
        return carry

    lax.fori_loop(0, 5, span_row, 0)

    for face, near, tiles, first_side in ((face0, near0, 6, 0), (face2, near2, 5, 4)):
        for side in range(2):
            code = codes[first_side + side]
            index, wall = code & 127, code >= WALL

            def local(t, carry, face=face, near=near, tiles=tiles, side=side, index=index, wall=wall):
                for q in range(2 * NV):
                    sign = -1.0 if 1 <= q <= 3 else 1.0
                    own = face[side, q * tiles + t]
                    near[side, q * tiles + t] = jnp.where(
                        wall, sign * own, take_lanes(face[1 - side, q * tiles + t], index)
                    )
                return carry

            lax.fori_loop(0, tiles, local, 0)


def surface_update(
    section, last, parity, codes, field, base, face0, face2, near0, near2, received,
    new_field, new_register, other0, other2, work,
):
    step = TIME_STEP
    flow_a, flow_b, span_a, span_b = received
    flow_odd, span_odd = parity[0], parity[1]
    for side, got in ((1 - flow_odd, flow_a), (flow_odd, flow_b)):
        code = codes[side]
        index = code & 127
        mask = (code & RECEIVED) != 0
        for g in range(4):
            shifted = index + 32 * g
            shifted = shifted & 127
            for t in range(15):
                other0[side, 15 * g + t] = jnp.where(
                    mask, take_lanes(got[t], shifted), near0[side, 15 * g + t]
                )
    for side, got in ((1 - span_odd, span_a), (span_odd, span_b)):
        code = codes[4 + side]
        index = code & 127
        mask = (code & RECEIVED) != 0
        for g in range(2):
            shifted = (index + 64 * g) & 127
            for t in range(25):
                other2[side, 25 * g + t] = jnp.where(
                    mask, take_lanes(got[t], shifted), near2[side, 25 * g + t]
                )

    def sides(own, other, tiles, t):
        result = []
        for side in range(2):
            result.append(
                (
                    [own[side, v * tiles + t] for v in range(NV)],
                    [own[side, (NV + v) * tiles + t] for v in range(NV)],
                    [other[side, v * tiles + t] for v in range(NV)],
                    [other[side, (NV + v) * tiles + t] for v in range(NV)],
                )
            )
        return result

    def span_row(chunk, carry):
        low, high = sides(face2, other2, 5, chunk)
        terms = face_terms(low, high, 2)
        for v in range(NV):
            values = [line_at(base, v, chunk, k) for k in range(6)]
            values = add_faces(values, terms, v, step)
            for k in range(6):
                put_line(work, v, chunk, k, values[k])
        return carry

    lax.fori_loop(0, 5, span_row, 0)

    def flow_row(j, carry):
        low, high = sides(face0, other0, 6, j)
        terms = face_terms(low, high, 0)
        for v in range(NV):
            rows = [v * VROWS + i * 48 + j * 8 for i in range(6)]
            values = add_faces([tile_at(work, row) for row in rows], terms, v, step)
            for i in range(6):
                updated = tile_at(field, rows[i]) + RK_B[section] * values[i]
                if last:
                    new_field[v, i, j] = updated[:6]
                    new_register[v, i, j] = values[i][:6]
                else:
                    put_tile(new_field, rows[i], updated)
                    put_tile(new_register, rows[i], values[i])
        return carry

    lax.fori_loop(0, 6, flow_row, 0)


def surface_kernel(
    section, parity, codes, field, base, face0, face2, near0, near2, ra, rb, rc, rd,
    new_field, new_register, new_face0, new_face2, flow_a, flow_b, span_a, span_b,
    other0, other2, work,
):
    surface_update(
        section, False, parity, codes, field, base, face0, face2, near0, near2, (ra, rb, rc, rd),
        new_field, new_register, other0, other2, work,
    )
    make_faces(new_field, new_face0, new_face2)
    pack_faces(parity, codes, new_face0, new_face2, flow_a, flow_b, span_a, span_b)


def last_kernel(
    section, parity, codes, field, base, face0, face2, near0, near2, ra, rb, rc, rd,
    advanced, register, other0, other2, work,
):
    surface_update(
        section, True, parity, codes, field, base, face0, face2, near0, near2, (ra, rb, rc, rd),
        advanced, register, other0, other2, work,
    )


def in_vmem(value):
    return pltpu.with_memory_space_constraint(value, pltpu.VMEM)


VMEM_SPEC = pl.BlockSpec(memory_space=pltpu.VMEM)
SMEM_SPEC = pl.BlockSpec(memory_space=pltpu.SMEM)
PARAMS = pltpu.CompilerParams(vmem_limit_bytes=32 * 1024 * 1024)


def vmem_out(shape, dtype=jnp.float32):
    return pltpu.VMEM(shape, dtype)


def face_outs():
    return [
        vmem_out(FACE0), vmem_out(FACE2), vmem_out(FLOW_PACK), vmem_out(FLOW_PACK),
        vmem_out(SPAN_PACK), vmem_out(SPAN_PACK),
    ]


def first_call(parity, conserved, lists):
    outs = [vmem_out(FIELD), vmem_out(CODES, jnp.int32)] + face_outs()
    return pl.pallas_call(
        first_kernel,
        out_shape=outs,
        in_specs=[SMEM_SPEC, VMEM_SPEC, VMEM_SPEC],
        out_specs=[VMEM_SPEC] * len(outs),
        compiler_params=PARAMS,
        name="first_faces",
    )(parity, conserved, lists)


def volume_call(section, field, register, codes, face0, face2):
    outs = [vmem_out(FIELD), vmem_out(FACE0), vmem_out(FACE2)]

    def kernel(*refs):
        if section > 0:
            volume_kernel(section, *refs)
        else:
            volume_kernel(section, refs[0], None, *refs[1:])

    args = [field, codes, face0, face2] if section == 0 else [field, register, codes, face0, face2]
    return pl.pallas_call(
        kernel,
        out_shape=outs,
        in_specs=[VMEM_SPEC] * len(args),
        out_specs=[VMEM_SPEC] * len(outs),
        scratch_shapes=[pltpu.VMEM((6 * VROWS, 128), jnp.float32)],
        compiler_params=PARAMS,
        cost_estimate=pl.CostEstimate(flops=10**7, bytes_accessed=4 * 10**6, transcendentals=0),
        name="volume",
    )(*map(in_vmem, args))


def surface_call(section, parity, *args):
    last = section == len(RK_A) - 1

    def kernel(*refs):
        (last_kernel if last else surface_kernel)(section, *refs)

    if last:
        outs = [jax.ShapeDtypeStruct((NV, 6, 6, 6, 128), jnp.float32)] * 2
    else:
        outs = [vmem_out(FIELD), vmem_out(FIELD)] + face_outs()
    return pl.pallas_call(
        kernel,
        out_shape=outs,
        in_specs=[SMEM_SPEC] + [VMEM_SPEC] * len(args),
        out_specs=[VMEM_SPEC] * len(outs),
        scratch_shapes=[
            pltpu.VMEM(FACE0, jnp.float32),
            pltpu.VMEM(FACE2, jnp.float32),
            pltpu.VMEM(FIELD, jnp.float32),
        ],
        compiler_params=PARAMS,
        name="surface",
    )(parity, *map(in_vmem, args))


def swap(value, axis, crossing):
    length = lax.axis_size(axis)
    if crossing:
        pairs = [(i, (i + 1) % length if i % 2 else (i - 1) % length) for i in range(length)]
    else:
        pairs = [(i, i ^ 1) for i in range(length)]
    return lax.ppermute(value, axis, pairs)


def body(conserved, flow_lists, span_lists, face_source):
    parity = jnp.stack([lax.axis_index("px") & 1, lax.axis_index("py") & 1]).astype(jnp.int32)
    lists = jnp.concatenate(
        [face_source, jnp.tile(flow_lists[0], (1, 4)), jnp.tile(span_lists[0], (1, 2))], axis=0
    )
    field, codes, face0, face2, *packs = first_call(parity, conserved, lists)
    register = None
    for section in range(len(RK_A)):
        flow_a, flow_b, span_a, span_b = packs
        rd = swap(span_b, "py", True)
        rc = swap(span_a, "py", False)
        rb = swap(flow_b, "px", True)
        ra = swap(flow_a, "px", False)
        base, near0, near2 = volume_call(section, field, register, codes, face0, face2)
        outs = surface_call(
            section, parity, codes, field, base, face0, face2, near0, near2, ra, rb, rc, rd
        )
        if section == len(RK_A) - 1:
            return tuple(outs)
        field, register, face0, face2, *packs = outs


def solution(mesh):
    return jax.shard_map(
        body,
        mesh=mesh,
        in_specs=(
            P(None, None, None, None, ("px", "py")),
            P(("px", "py"), None, None),
            P(("px", "py"), None, None),
            P(None, ("px", "py")),
        ),
        out_specs=(
            P(None, None, None, None, ("px", "py")),
            P(None, None, None, None, ("px", "py")),
        ),
        check_vma=False,
    )
```

profile of v0, /device:TPU:1, one launch (start us, length us, event | category | flops | bytes accessed | tf_op | source)
XLA Modules:
  0.0 65.3 jit_solution(15541767320156836440)
XLA Ops:
  2.9 1.1 %copy-done = f32[5,6,6,6,128]{4,3,2,1,0:T(8,128)S(1)} copy-done((f32[5,6,6,6,128]{4,3,2,1,0:T(8,128)S(1)}, f32[5,6,6,6,128]{4,3,2,1,0:T(8,128)}, u32[]{:S(2)}) %copy-start) | copy-done | bytes 552984
  4.0 1.2 %first_faces.1 = (f32[1600,128]{1,0:T(8,128)S(1)}, s32[10,8,128]{2,1,0:T(8,128)S(1)}, f32[2,60,8,128]{3,2,1,0:T(8,128)S(1)}, f32[2,50,8,128]{3,2,1,0:T(8,128)S(1...) custom-call(s32[2]{0:T(128)S(1)} %pad_add_fusion.1.parity.refs_0_, ...), custom_call_target="tpu_custom_call" | custom-call | tf_op jit(solution)/shard_map/first_faces/pallas_call | solution.py:471
  5.2 2.2 %collective-permute-start.2 = (f32[25,8,128]{2,1,0:T(8,128)S(1)}, f32[25,8,128]{2,1,0:T(8,128)S(1)}, u32[]{:S(2)}, u32[]{:S(2)}) collective-permute-start(f32[25,8,128]{2,1,0:T(8,128)S(1)} %get-tuple-element.66), channel_id=1, source_target_pairs={{0,1},{1,0},{2,3},{3,2},{4,5},{5,4},{6,7},{7,6},{8,9},{9,8},{10,11... | collective-permute-start | bytes 307208 | tf_op jit(solution)/shard_map/ppermute | solution.py:534
  7.4 5.4 %collective-permute-start.3 = (f32[25,8,128]{2,1,0:T(8,128)S(1)}, f32[25,8,128]{2,1,0:T(8,128)S(1)}, u32[]{:S(2)}, u32[]{:S(2)}) collective-permute-start(f32[25,8,128]{2,1,0:T(8,128)S(1)} %get-tuple-element.67), channel_id=1, source_target_pairs={{0,15},{1,2},{2,1},{3,4},{4,3},{5,6},{6,5},{7,8},{8,7},{9,10},{10,... | collective-permute-start | bytes 307208 | tf_op jit(solution)/shard_map/ppermute | solution.py:534
  12.7 1.2 %collective-permute-start = (f32[15,8,128]{2,1,0:T(8,128)S(1)}, f32[15,8,128]{2,1,0:T(8,128)S(1)}, u32[]{:S(2)}, u32[]{:S(2)}) collective-permute-start(f32[15,8,128]{2,1,0:T(8,128)S(1)} %get-tuple-element.64), channel_id=1, source_target_pairs={{0,16},{16,0},{32,48},{48,32},{64,80},{80,64},{96,112},{112,96},{1... | collective-permute-start | bytes 184328 | tf_op jit(solution)/shard_map/ppermute | solution.py:534
  14.0 1.1 %collective-permute-start.1 = (f32[15,8,128]{2,1,0:T(8,128)S(1)}, f32[15,8,128]{2,1,0:T(8,128)S(1)}, u32[]{:S(2)}, u32[]{:S(2)}) collective-permute-start(f32[15,8,128]{2,1,0:T(8,128)S(1)} %get-tuple-element.65), channel_id=1, source_target_pairs={{0,112},{16,32},{32,16},{48,64},{64,48},{80,96},{96,80},{112,0},{1... | collective-permute-start | bytes 184328 | tf_op jit(solution)/shard_map/ppermute | solution.py:534
  15.1 4.1 %volume.5 = (f32[1600,128]{1,0:T(8,128)S(1)}, f32[2,60,8,128]{3,2,1,0:T(8,128)S(1)}, f32[2,50,8,128]{3,2,1,0:T(8,128)S(1)}) custom-call(f32[1600,128]{1,0:T(8,128)S(1)} %get-tuple-element.58.refs_0_.refs_2_, s32[10,8,128]{2,1,0:T(8,128)S(1)} %get-tuple-element.57.refs_1_.refs_2_, f32[2,60,8,128]{3,2,1,0:T(8,128)S(1)} %get-tuple-element.59.refs_2_.refs_4_, ...), custom_call_target="tpu_custom_call" | custom-call | flops 10000000 | bytes 4000000 | tf_op jit(solution)/shard_map/volume/pallas_call | solution.py:491
  19.3 2.2 %surface.5 = (f32[1600,128]{1,0:T(8,128)S(1)}, f32[1600,128]{1,0:T(8,128)S(1)}, f32[2,60,8,128]{3,2,1,0:T(8,128)S(1)}, f32[2,50,8,128]{3,2,1,0:T(8,128)S(1)}, f3...) custom-call(s32[2]{0:T(128)S(1)} %pad_add_fusion.1.parity.refs_0_, ...), custom_call_target="tpu_custom_call" | custom-call | tf_op jit(solution)/shard_map/surface/pallas_call | solution.py:513
  22.3 2.3 %collective-permute-start.4 = (f32[15,8,128]{2,1,0:T(8,128)S(1)}, f32[15,8,128]{2,1,0:T(8,128)S(1)}, u32[]{:S(2)}, u32[]{:S(2)}) collective-permute-start(f32[15,8,128]{2,1,0:T(8,128)S(1)} %get-tuple-element.75), channel_id=1, source_target_pairs={{0,16},{16,0},{32,48},{48,32},{64,80},{80,64},{96,112},{112,96},{1... | collective-permute-start | bytes 184328 | tf_op jit(solution)/shard_map/ppermute | solution.py:534
  24.6 0.8 %collective-permute-start.5 = (f32[15,8,128]{2,1,0:T(8,128)S(1)}, f32[15,8,128]{2,1,0:T(8,128)S(1)}, u32[]{:S(2)}, u32[]{:S(2)}) collective-permute-start(f32[15,8,128]{2,1,0:T(8,128)S(1)} %get-tuple-element.76), channel_id=1, source_target_pairs={{0,112},{16,32},{32,16},{48,64},{64,48},{80,96},{96,80},{112,0},{1... | collective-permute-start | bytes 184328 | tf_op jit(solution)/shard_map/ppermute | solution.py:534
  25.4 4.2 %volume.6 = (f32[1600,128]{1,0:T(8,128)S(1)}, f32[2,60,8,128]{3,2,1,0:T(8,128)S(1)}, f32[2,50,8,128]{3,2,1,0:T(8,128)S(1)}) custom-call(f32[1600,128]{1,0:T(8,128)S(1)} %get-tuple-element.68.refs_0_.refs_2_, f32[1600,128]{1,0:T(8,128)S(1)} %get-tuple-element.69.refs_1_, s32[10,8,128]{2,1,0:T(8,128)S(1)} %get-tuple-element.57.refs_1_.refs_2_, ...), custom_call_target="tpu_custom_call" | custom-call | flops 10000000 | bytes 4000000 | tf_op jit(solution)/shard_map/volume/pallas_call | solution.py:491
  29.7 2.2 %surface.6 = (f32[1600,128]{1,0:T(8,128)S(1)}, f32[1600,128]{1,0:T(8,128)S(1)}, f32[2,60,8,128]{3,2,1,0:T(8,128)S(1)}, f32[2,50,8,128]{3,2,1,0:T(8,128)S(1)}, f3...) custom-call(s32[2]{0:T(128)S(1)} %pad_add_fusion.1.parity.refs_0_, ...), custom_call_target="tpu_custom_call" | custom-call | tf_op jit(solution)/shard_map/surface/pallas_call | solution.py:513
  31.9 3.1 %collective-permute-start.11 = (f32[25,8,128]{2,1,0:T(8,128)S(1)}, f32[25,8,128]{2,1,0:T(8,128)S(1)}, u32[]{:S(2)}, u32[]{:S(2)}) collective-permute-start(f32[25,8,128]{2,1,0:T(8,128)S(1)} %get-tuple-element.89), channel_id=1, source_target_pairs={{0,15},{1,2},{2,1},{3,4},{4,3},{5,6},{6,5},{7,8},{8,7},{9,10},{10,... | collective-permute-start | bytes 307208 | tf_op jit(solution)/shard_map/ppermute | solution.py:534
  35.1 1.2 %collective-permute-start.8 = (f32[15,8,128]{2,1,0:T(8,128)S(1)}, f32[15,8,128]{2,1,0:T(8,128)S(1)}, u32[]{:S(2)}, u32[]{:S(2)}) collective-permute-start(f32[15,8,128]{2,1,0:T(8,128)S(1)} %get-tuple-element.86), channel_id=1, source_target_pairs={{0,16},{16,0},{32,48},{48,32},{64,80},{80,64},{96,112},{112,96},{1... | collective-permute-start | bytes 184328 | tf_op jit(solution)/shard_map/ppermute | solution.py:534
  37.1 4.2 %volume.7 = (f32[1600,128]{1,0:T(8,128)S(1)}, f32[2,60,8,128]{3,2,1,0:T(8,128)S(1)}, f32[2,50,8,128]{3,2,1,0:T(8,128)S(1)}) custom-call(f32[1600,128]{1,0:T(8,128)S(1)} %get-tuple-element.79.refs_0_.refs_2_, f32[1600,128]{1,0:T(8,128)S(1)} %get-tuple-element.80.refs_1_, s32[10,8,128]{2,1,0:T(8,128)S(1)} %get-tuple-element.57.refs_1_.refs_2_, ...), custom_call_target="tpu_custom_call" | custom-call | flops 10000000 | bytes 4000000 | tf_op jit(solution)/shard_map/volume/pallas_call | solution.py:491
  41.4 2.2 %surface.7 = (f32[1600,128]{1,0:T(8,128)S(1)}, f32[1600,128]{1,0:T(8,128)S(1)}, f32[2,60,8,128]{3,2,1,0:T(8,128)S(1)}, f32[2,50,8,128]{3,2,1,0:T(8,128)S(1)}, f3...) custom-call(s32[2]{0:T(128)S(1)} %pad_add_fusion.1.parity.refs_0_, ...), custom_call_target="tpu_custom_call" | custom-call | tf_op jit(solution)/shard_map/surface/pallas_call | solution.py:513
  43.6 1.8 %collective-permute-start.15 = (f32[25,8,128]{2,1,0:T(8,128)S(1)}, f32[25,8,128]{2,1,0:T(8,128)S(1)}, u32[]{:S(2)}, u32[]{:S(2)}) collective-permute-start(f32[25,8,128]{2,1,0:T(8,128)S(1)} %get-tuple-element.100), channel_id=1, source_target_pairs={{0,15},{1,2},{2,1},{3,4},{4,3},{5,6},{6,5},{7,8},{8,7},{9,10},{10,... | collective-permute-start | bytes 307208 | tf_op jit(solution)/shard_map/ppermute | solution.py:534
  45.5 1.5 %collective-permute-start.12 = (f32[15,8,128]{2,1,0:T(8,128)S(1)}, f32[15,8,128]{2,1,0:T(8,128)S(1)}, u32[]{:S(2)}, u32[]{:S(2)}) collective-permute-start(f32[15,8,128]{2,1,0:T(8,128)S(1)} %get-tuple-element.97), channel_id=1, source_target_pairs={{0,16},{16,0},{32,48},{48,32},{64,80},{80,64},{96,112},{112,96},{1... | collective-permute-start | bytes 184328 | tf_op jit(solution)/shard_map/ppermute | solution.py:534
  47.5 4.2 %volume.8 = (f32[1600,128]{1,0:T(8,128)S(1)}, f32[2,60,8,128]{3,2,1,0:T(8,128)S(1)}, f32[2,50,8,128]{3,2,1,0:T(8,128)S(1)}) custom-call(f32[1600,128]{1,0:T(8,128)S(1)} %get-tuple-element.90.refs_0_.refs_2_, f32[1600,128]{1,0:T(8,128)S(1)} %get-tuple-element.91.refs_1_, s32[10,8,128]{2,1,0:T(8,128)S(1)} %get-tuple-element.57.refs_1_.refs_2_, ...), custom_call_target="tpu_custom_call" | custom-call | flops 10000000 | bytes 4000000 | tf_op jit(solution)/shard_map/volume/pallas_call | solution.py:491
  51.8 2.2 %surface.8 = (f32[1600,128]{1,0:T(8,128)S(1)}, f32[1600,128]{1,0:T(8,128)S(1)}, f32[2,60,8,128]{3,2,1,0:T(8,128)S(1)}, f32[2,50,8,128]{3,2,1,0:T(8,128)S(1)}, f3...) custom-call(s32[2]{0:T(128)S(1)} %pad_add_fusion.1.parity.refs_0_, ...), custom_call_target="tpu_custom_call" | custom-call | tf_op jit(solution)/shard_map/surface/pallas_call | solution.py:513
  54.0 2.3 %collective-permute-start.19 = (f32[25,8,128]{2,1,0:T(8,128)S(1)}, f32[25,8,128]{2,1,0:T(8,128)S(1)}, u32[]{:S(2)}, u32[]{:S(2)}) collective-permute-start(f32[25,8,128]{2,1,0:T(8,128)S(1)} %get-tuple-element.111), channel_id=1, source_target_pairs={{0,15},{1,2},{2,1},{3,4},{4,3},{5,6},{6,5},{7,8},{8,7},{9,10},{10,... | collective-permute-start | bytes 307208 | tf_op jit(solution)/shard_map/ppermute | solution.py:534
  56.3 1.3 %collective-permute-start.16 = (f32[15,8,128]{2,1,0:T(8,128)S(1)}, f32[15,8,128]{2,1,0:T(8,128)S(1)}, u32[]{:S(2)}, u32[]{:S(2)}) collective-permute-start(f32[15,8,128]{2,1,0:T(8,128)S(1)} %get-tuple-element.108), channel_id=1, source_target_pairs={{0,16},{16,0},{32,48},{48,32},{64,80},{80,64},{96,112},{112,96},{1... | collective-permute-start | bytes 184328 | tf_op jit(solution)/shard_map/ppermute | solution.py:534
  58.4 4.2 %volume.9 = (f32[1600,128]{1,0:T(8,128)S(1)}, f32[2,60,8,128]{3,2,1,0:T(8,128)S(1)}, f32[2,50,8,128]{3,2,1,0:T(8,128)S(1)}) custom-call(f32[1600,128]{1,0:T(8,128)S(1)} %get-tuple-element.101.refs_0_.refs_2_, f32[1600,128]{1,0:T(8,128)S(1)} %get-tuple-element.102.refs_1_, s32[10,8,128]{2,1,0:T(8,128)S(1)} %get-tuple-element.57.refs_1_.refs_2_, ...), custom_call_target="tpu_custom_call" | custom-call | flops 10000000 | bytes 4000000 | tf_op jit(solution)/shard_map/volume/pallas_call | solution.py:491
  62.6 2.7 %surface.9 = (f32[5,6,6,6,128]{4,3,2,1,0:T(8,128)}, f32[5,6,6,6,128]{4,3,2,1,0:T(8,128)}) custom-call(s32[2]{0:T(128)S(1)} %pad_add_fusion.1.parity.refs_0_, s32[10,8,128]{2,1,0:T(8,128)S(1)} %get-tuple-element.57.refs_1_.refs_2_, f32[1600,128]{1,0:T(8,128)S(1)} %get-tuple-element.101.refs_0_.refs_2_, f32[1600,128]{1,0:T(8,128)S(1)} %get-tuple-element.105.refs_3_, ...), custom_call_target="tpu_custom_call" | custom-call | tf_op jit(solution)/shard_map/surface/pallas_call | solution.py:513
  (41 shorter events, 5.4 us)
Async XLA Ops:
  0.6 0.7 %copy-start.2 = (s32[1,2,64]{2,1,0:T(2,128)S(1)}, s32[1,2,64]{2,1,0:T(2,128)}, u32[]{:S(2)}) copy-start(s32[1,2,64]{2,1,0:T(2,128)} %param.6) | copy-start | bytes 1540
  1.4 0.7 %copy-start.3 = (s32[1,2,32]{2,1,0:T(2,128)S(1)}, s32[1,2,32]{2,1,0:T(2,128)}, u32[]{:S(2)}) copy-start(s32[1,2,32]{2,1,0:T(2,128)} %param.5) | copy-start | bytes 772
  2.2 0.7 %copy-start.1 = (s32[6,128]{1,0:T(8,128)S(1)}, s32[6,128]{1,0:T(8,128)}, u32[]{:S(2)}) copy-start(s32[6,128]{1,0:T(8,128)} %param.7) | copy-start | bytes 9220
  2.9 1.1 %copy-start = (f32[5,6,6,6,128]{4,3,2,1,0:T(8,128)S(1)}, f32[5,6,6,6,128]{4,3,2,1,0:T(8,128)}, u32[]{:S(2)}) copy-start(f32[5,6,6,6,128]{4,3,2,1,0:T(8,128)} %conserved.1) | copy-start | bytes 1658884
  5.2 14.1 %collective-permute-start.2 = (f32[25,8,128]{2,1,0:T(8,128)S(1)}, f32[25,8,128]{2,1,0:T(8,128)S(1)}, u32[]{:S(2)}, u32[]{:S(2)}) collective-permute-start(f32[25,8,128]{2,1,0:T(8,128)S(1)} %get-tuple-element.66), channel_id=1, source_target_pairs={{0,1},{1,0},{2,3},{3,2},{4,5},{5,4},{6,7},{7,6},{8,9},{9,8},{10,11... | collective-permute-start | bytes 307208 | tf_op jit(solution)/shard_map/ppermute | solution.py:534
  7.4 11.9 %collective-permute-start.3 = (f32[25,8,128]{2,1,0:T(8,128)S(1)}, f32[25,8,128]{2,1,0:T(8,128)S(1)}, u32[]{:S(2)}, u32[]{:S(2)}) collective-permute-start(f32[25,8,128]{2,1,0:T(8,128)S(1)} %get-tuple-element.67), channel_id=1, source_target_pairs={{0,15},{1,2},{2,1},{3,4},{4,3},{5,6},{6,5},{7,8},{8,7},{9,10},{10,... | collective-permute-start | bytes 307208 | tf_op jit(solution)/shard_map/ppermute | solution.py:534
  12.7 6.5 %collective-permute-start = (f32[15,8,128]{2,1,0:T(8,128)S(1)}, f32[15,8,128]{2,1,0:T(8,128)S(1)}, u32[]{:S(2)}, u32[]{:S(2)}) collective-permute-start(f32[15,8,128]{2,1,0:T(8,128)S(1)} %get-tuple-element.64), channel_id=1, source_target_pairs={{0,16},{16,0},{32,48},{48,32},{64,80},{80,64},{96,112},{112,96},{1... | collective-permute-start | bytes 184328 | tf_op jit(solution)/shard_map/ppermute | solution.py:534
  14.0 5.3 %collective-permute-start.1 = (f32[15,8,128]{2,1,0:T(8,128)S(1)}, f32[15,8,128]{2,1,0:T(8,128)S(1)}, u32[]{:S(2)}, u32[]{:S(2)}) collective-permute-start(f32[15,8,128]{2,1,0:T(8,128)S(1)} %get-tuple-element.65), channel_id=1, source_target_pairs={{0,112},{16,32},{32,16},{48,64},{64,48},{80,96},{96,80},{112,0},{1... | collective-permute-start | bytes 184328 | tf_op jit(solution)/shard_map/ppermute | solution.py:534
  21.5 8.2 %collective-permute-start.6 = (f32[25,8,128]{2,1,0:T(8,128)S(1)}, f32[25,8,128]{2,1,0:T(8,128)S(1)}, u32[]{:S(2)}, u32[]{:S(2)}) collective-permute-start(f32[25,8,128]{2,1,0:T(8,128)S(1)} %get-tuple-element.77), channel_id=1, source_target_pairs={{0,1},{1,0},{2,3},{3,2},{4,5},{5,4},{6,7},{7,6},{8,9},{9,8},{10,11... | collective-permute-start | bytes 307208 | tf_op jit(solution)/shard_map/ppermute | solution.py:534
  21.6 8.1 %collective-permute-start.7 = (f32[25,8,128]{2,1,0:T(8,128)S(1)}, f32[25,8,128]{2,1,0:T(8,128)S(1)}, u32[]{:S(2)}, u32[]{:S(2)}) collective-permute-start(f32[25,8,128]{2,1,0:T(8,128)S(1)} %get-tuple-element.78), channel_id=1, source_target_pairs={{0,15},{1,2},{2,1},{3,4},{4,3},{5,6},{6,5},{7,8},{8,7},{9,10},{10,... | collective-permute-start | bytes 307208 | tf_op jit(solution)/shard_map/ppermute | solution.py:534
  22.3 7.4 %collective-permute-start.4 = (f32[15,8,128]{2,1,0:T(8,128)S(1)}, f32[15,8,128]{2,1,0:T(8,128)S(1)}, u32[]{:S(2)}, u32[]{:S(2)}) collective-permute-start(f32[15,8,128]{2,1,0:T(8,128)S(1)} %get-tuple-element.75), channel_id=1, source_target_pairs={{0,16},{16,0},{32,48},{48,32},{64,80},{80,64},{96,112},{112,96},{1... | collective-permute-start | bytes 184328 | tf_op jit(solution)/shard_map/ppermute | solution.py:534
  24.6 5.0 %collective-permute-start.5 = (f32[15,8,128]{2,1,0:T(8,128)S(1)}, f32[15,8,128]{2,1,0:T(8,128)S(1)}, u32[]{:S(2)}, u32[]{:S(2)}) collective-permute-start(f32[15,8,128]{2,1,0:T(8,128)S(1)} %get-tuple-element.76), channel_id=1, source_target_pairs={{0,112},{16,32},{32,16},{48,64},{64,48},{80,96},{96,80},{112,0},{1... | collective-permute-start | bytes 184328 | tf_op jit(solution)/shard_map/ppermute | solution.py:534
  31.9 9.5 %collective-permute-start.10 = (f32[25,8,128]{2,1,0:T(8,128)S(1)}, f32[25,8,128]{2,1,0:T(8,128)S(1)}, u32[]{:S(2)}, u32[]{:S(2)}) collective-permute-start(f32[25,8,128]{2,1,0:T(8,128)S(1)} %get-tuple-element.88), channel_id=1, source_target_pairs={{0,1},{1,0},{2,3},{3,2},{4,5},{5,4},{6,7},{7,6},{8,9},{9,8},{10,11... | collective-permute-start | bytes 307208 | tf_op jit(solution)/shard_map/ppermute | solution.py:534
  31.9 9.4 %collective-permute-start.11 = (f32[25,8,128]{2,1,0:T(8,128)S(1)}, f32[25,8,128]{2,1,0:T(8,128)S(1)}, u32[]{:S(2)}, u32[]{:S(2)}) collective-permute-start(f32[25,8,128]{2,1,0:T(8,128)S(1)} %get-tuple-element.89), channel_id=1, source_target_pairs={{0,15},{1,2},{2,1},{3,4},{4,3},{5,6},{6,5},{7,8},{8,7},{9,10},{10,... | collective-permute-start | bytes 307208 | tf_op jit(solution)/shard_map/ppermute | solution.py:534
  35.1 6.2 %collective-permute-start.8 = (f32[15,8,128]{2,1,0:T(8,128)S(1)}, f32[15,8,128]{2,1,0:T(8,128)S(1)}, u32[]{:S(2)}, u32[]{:S(2)}) collective-permute-start(f32[15,8,128]{2,1,0:T(8,128)S(1)} %get-tuple-element.86), channel_id=1, source_target_pairs={{0,16},{16,0},{32,48},{48,32},{64,80},{80,64},{96,112},{112,96},{1... | collective-permute-start | bytes 184328 | tf_op jit(solution)/shard_map/ppermute | solution.py:534
  36.3 5.0 %collective-permute-start.9 = (f32[15,8,128]{2,1,0:T(8,128)S(1)}, f32[15,8,128]{2,1,0:T(8,128)S(1)}, u32[]{:S(2)}, u32[]{:S(2)}) collective-permute-start(f32[15,8,128]{2,1,0:T(8,128)S(1)} %get-tuple-element.87), channel_id=1, source_target_pairs={{0,112},{16,32},{32,16},{48,64},{64,48},{80,96},{96,80},{112,0},{1... | collective-permute-start | bytes 184328 | tf_op jit(solution)/shard_map/ppermute | solution.py:534
  43.5 8.2 %collective-permute-start.14 = (f32[25,8,128]{2,1,0:T(8,128)S(1)}, f32[25,8,128]{2,1,0:T(8,128)S(1)}, u32[]{:S(2)}, u32[]{:S(2)}) collective-permute-start(f32[25,8,128]{2,1,0:T(8,128)S(1)} %get-tuple-element.99), channel_id=1, source_target_pairs={{0,1},{1,0},{2,3},{3,2},{4,5},{5,4},{6,7},{7,6},{8,9},{9,8},{10,11... | collective-permute-start | bytes 307208 | tf_op jit(solution)/shard_map/ppermute | solution.py:534
  43.6 8.1 %collective-permute-start.15 = (f32[25,8,128]{2,1,0:T(8,128)S(1)}, f32[25,8,128]{2,1,0:T(8,128)S(1)}, u32[]{:S(2)}, u32[]{:S(2)}) collective-permute-start(f32[25,8,128]{2,1,0:T(8,128)S(1)} %get-tuple-element.100), channel_id=1, source_target_pairs={{0,15},{1,2},{2,1},{3,4},{4,3},{5,6},{6,5},{7,8},{8,7},{9,10},{10,... | collective-permute-start | bytes 307208 | tf_op jit(solution)/shard_map/ppermute | solution.py:534
  45.5 6.2 %collective-permute-start.12 = (f32[15,8,128]{2,1,0:T(8,128)S(1)}, f32[15,8,128]{2,1,0:T(8,128)S(1)}, u32[]{:S(2)}, u32[]{:S(2)}) collective-permute-start(f32[15,8,128]{2,1,0:T(8,128)S(1)} %get-tuple-element.97), channel_id=1, source_target_pairs={{0,16},{16,0},{32,48},{48,32},{64,80},{80,64},{96,112},{112,96},{1... | collective-permute-start | bytes 184328 | tf_op jit(solution)/shard_map/ppermute | solution.py:534
  47.0 4.7 %collective-permute-start.13 = (f32[15,8,128]{2,1,0:T(8,128)S(1)}, f32[15,8,128]{2,1,0:T(8,128)S(1)}, u32[]{:S(2)}, u32[]{:S(2)}) collective-permute-start(f32[15,8,128]{2,1,0:T(8,128)S(1)} %get-tuple-element.98), channel_id=1, source_target_pairs={{0,112},{16,32},{32,16},{48,64},{64,48},{80,96},{96,80},{112,0},{1... | collective-permute-start | bytes 184328 | tf_op jit(solution)/shard_map/ppermute | solution.py:534
  53.9 8.6 %collective-permute-start.18 = (f32[25,8,128]{2,1,0:T(8,128)S(1)}, f32[25,8,128]{2,1,0:T(8,128)S(1)}, u32[]{:S(2)}, u32[]{:S(2)}) collective-permute-start(f32[25,8,128]{2,1,0:T(8,128)S(1)} %get-tuple-element.110), channel_id=1, source_target_pairs={{0,1},{1,0},{2,3},{3,2},{4,5},{5,4},{6,7},{7,6},{8,9},{9,8},{10,11... | collective-permute-start | bytes 307208 | tf_op jit(solution)/shard_map/ppermute | solution.py:534
  54.0 8.6 %collective-permute-start.19 = (f32[25,8,128]{2,1,0:T(8,128)S(1)}, f32[25,8,128]{2,1,0:T(8,128)S(1)}, u32[]{:S(2)}, u32[]{:S(2)}) collective-permute-start(f32[25,8,128]{2,1,0:T(8,128)S(1)} %get-tuple-element.111), channel_id=1, source_target_pairs={{0,15},{1,2},{2,1},{3,4},{4,3},{5,6},{6,5},{7,8},{8,7},{9,10},{10,... | collective-permute-start | bytes 307208 | tf_op jit(solution)/shard_map/ppermute | solution.py:534
  56.3 6.2 %collective-permute-start.16 = (f32[15,8,128]{2,1,0:T(8,128)S(1)}, f32[15,8,128]{2,1,0:T(8,128)S(1)}, u32[]{:S(2)}, u32[]{:S(2)}) collective-permute-start(f32[15,8,128]{2,1,0:T(8,128)S(1)} %get-tuple-element.108), channel_id=1, source_target_pairs={{0,16},{16,0},{32,48},{48,32},{64,80},{80,64},{96,112},{112,96},{1... | collective-permute-start | bytes 184328 | tf_op jit(solution)/shard_map/ppermute | solution.py:534
  57.6 5.0 %collective-permute-start.17 = (f32[15,8,128]{2,1,0:T(8,128)S(1)}, f32[15,8,128]{2,1,0:T(8,128)S(1)}, u32[]{:S(2)}, u32[]{:S(2)}) collective-permute-start(f32[15,8,128]{2,1,0:T(8,128)S(1)} %get-tuple-element.109), channel_id=1, source_target_pairs={{0,112},{16,32},{32,16},{48,64},{64,48},{80,96},{96,80},{112,0},{1... | collective-permute-start | bytes 184328 | tf_op jit(solution)/shard_map/ppermute | solution.py:534
where the time goes:
time: 65.5 us; the launch traced here: 65.3 us
  Pallas kernels  33.6 us (51%)
  starting transfers between devices  27.5 us (42%)
  local copies, waits for them, and re-layouts  3.25 us (5%)
  between operations  0.89 us (1%)
    ppermute x20, starting transfers between devices, swap(): return lax.ppermute(value, axis, pairs)  27.5 us
    pallas_call x5, Pallas kernels, volume_call(): pl.pallas_call(kernel, out_shape=outs, in_specs=[VMEM_SPEC] * len(args),...  20.9 us
    pallas_call x5, Pallas kernels, surface_call(): pl.pallas_call(kernel, out_shape=outs, in_specs=[SMEM_SPEC] + [VMEM_SPEC]...  11.5 us
    unnamed x8, local copies, waits for them, and re-layouts  3.08 us
  transfers between devices with their start and end apart: 20, of which 0 were waited for; matrix products, arithmetic and copies ran while one was open for 0% of the time, Pallas kernels for 32%

commit v1 on v0

--- a/solution.py
+++ b/solution.py
@@ -52,6 +52,8 @@
 FACE2 = (2, 50, 8, 128)
 FLOW_PACK = (15, 8, 128)
 SPAN_PACK = (25, 8, 128)
+FLOW_FAR = (16, 8, 128)
+SPAN_FAR = (26, 8, 128)
 CODES = (10, 8, 128)
 RECEIVED = 256
 WALL = 512
@@ -191,6 +193,11 @@
 
 
 def make_faces(field, face0, face2):
+    faces_flow(field, face0)
+    faces_span(field, face2)
+
+
+def faces_flow(field, face0):
     def flow_row(j, carry):
         for v in range(NV):
             values = [tile_at(field, v * VROWS + i * 48 + j * 8) for i in range(6)]
@@ -203,6 +210,8 @@
 
     lax.fori_loop(0, 6, flow_row, 0)
 
+
+def faces_span(field, face2):
     def span_row(chunk, carry):
         for v in range(NV):
             values = [line_at(field, v, chunk, k) for k in range(6)]
@@ -216,9 +225,15 @@
     lax.fori_loop(0, 5, span_row, 0)
 
 
-def pack_faces(parity, codes, face0, face2, flow_a, flow_b, span_a, span_b):
+def pack_faces(codes, face0, face2, flow_a, flow_b, span_a, span_b):
     lane = lax.broadcasted_iota(jnp.int32, (8, 128), 1)
-    flow_odd, span_odd = parity[0], parity[1]
+    flow_odd, span_odd = lax.axis_index("px") & 1, lax.axis_index("py") & 1
+    for side, out in ((1 - span_odd, span_a), (span_odd, span_b)):
+        index = codes[8 + side]
+        for t in range(25):
+            out[t] = jnp.where(
+                lane >= 64, take_lanes(face2[side, 25 + t], index), take_lanes(face2[side, t], index)
+            )
     for side, out in ((1 - flow_odd, flow_a), (flow_odd, flow_b)):
         index = codes[6 + side]
         for t in range(15):
@@ -226,23 +241,25 @@
             for g in range(1, 4):
                 packed = jnp.where(lane >= 32 * g, take_lanes(face0[side, 15 * g + t], index), packed)
             out[t] = packed
-    for side, out in ((1 - span_odd, span_a), (span_odd, span_b)):
-        index = codes[8 + side]
-        for t in range(25):
-            out[t] = jnp.where(
-                lane >= 64, take_lanes(face2[side, 25 + t], index), take_lanes(face2[side, t], index)
-            )
 
 
 def first_kernel(
-    parity, conserved, lists, field, codes, face0, face2, flow_a, flow_b, span_a, span_b
+    conserved, flow_lists, span_lists, face_source, field, codes, face0, face2,
+    flow_a, flow_b, span_a, span_b, state, flow_rows, span_rows, columns, list_sems, state_sems,
 ):
-    for v in range(NV):
-        for i in range(6):
-            for j in range(6):
-                field[pl.ds(v * VROWS + i * 48 + j * 8, 6), :] = conserved[v, i, j]
+    copies = [
+        pltpu.make_async_copy(source, target, list_sems.at[n])
+        for n, (source, target) in enumerate(
+            ((flow_lists, flow_rows), (span_lists, span_rows), (face_source, columns))
+        )
+    ]
+    copies += [pltpu.make_async_copy(conserved.at[v], state.at[v], state_sems.at[v]) for v in range(NV)]
+    for copy in copies:
+        copy.start()
+    for copy in copies[:3]:
+        copy.wait()
     for side in range(6):
-        column = lists[pl.ds(side, 1), :]
+        column = columns[pl.ds(side, 1), :]
         mask = 31 if side < 2 else 63
         offset = 768 if side < 2 else 832
         code = jnp.where(
@@ -251,15 +268,38 @@
             jnp.where(column < 960, ((column - offset) & mask) + RECEIVED, WALL),
         )
         codes[side] = jnp.broadcast_to(code, (8, 128))
-    for row in range(6, 10):
-        codes[row] = jnp.broadcast_to(lists[pl.ds(row, 1), :], (8, 128))
+    for side in range(2):
+        flow_row = jnp.concatenate([flow_rows[0, pl.ds(side, 1), :]] * 4, axis=1)
+        span_row = jnp.concatenate([span_rows[0, pl.ds(side, 1), :]] * 2, axis=1)
+        codes[6 + side] = jnp.broadcast_to(flow_row, (8, 128))
+        codes[8 + side] = jnp.broadcast_to(span_row, (8, 128))
+    for v in range(NV):
+        copies[3 + v].wait()
+        for i in range(6):
+            for j in range(6):
+                field[pl.ds(v * VROWS + i * 48 + j * 8, 6), :] = state[v, i, j]
     make_faces(field, face0, face2)
-    pack_faces(parity, codes, face0, face2, flow_a, flow_b, span_a, span_b)
-
-
-def volume_kernel(section, field, register, codes, face0, face2, base, near0, near2, prims):
-    step = TIME_STEP
-
+    pack_faces(codes, face0, face2, flow_a, flow_b, span_a, span_b)
+
+
+def volume_kernel(
+    section, field, register, codes, face0, face2, base, near0, near2, prims, face1, near1
+):
+    volume_primitives(field, prims)
+    wall_faces(field, face1)
+    volume_flow(section, field, register, codes, base, prims, face1, near1)
+    volume_wall(field, codes, base, prims, face1, near1, face0, near0)
+    volume_span(field, codes, base, prims, face2, near2)
+
+
+def take_local(codes, first_side, face, near, tiles, t):
+    for side in range(2):
+        index = codes[first_side + side] & 127
+        for q in range(2 * NV):
+            near[side, q * tiles + t] = take_lanes(face[1 - side, q * tiles + t], index)
+
+
+def volume_primitives(field, prims):
     def primitives(n, carry):
         for u in range(4):
             row = (n * 4 + u) * 8
@@ -270,9 +310,9 @@
 
     lax.fori_loop(0, 9, primitives, 0)
 
-    def viscous_and_flux(lines, nodes, direction, var, sums):
-        second = second_derivative(lines[var], step * VISCOSITY)
-        return [second[i] - float(step / WEIGHTS[i]) * sums[i][var] for i in range(6)]
+
+def volume_flow(section, field, register, codes, base, prims, face1, near1):
+    step = TIME_STEP
 
     def flow_row(j, carry):
         row = j * 8
@@ -286,39 +326,51 @@
                 if section > 0:
                     value = value + RK_A[section] * tile_at(register, v * VROWS + i * 48 + row)
                 put_tile(base, v * VROWS + i * 48 + row, value)
+        take_local(codes, 2, face1, near1, 6, j)
         return carry
 
     lax.fori_loop(0, 6, flow_row, 0)
 
-    low_code, high_code = codes[2], codes[3]
-    low_index, high_index = low_code & 127, high_code & 127
-    low_wall, high_wall = low_code >= WALL, high_code >= WALL
+
+def wall_faces(field, face1):
+    def wall_row(i, carry):
+        for v in range(NV):
+            values = [tile_at(field, v * VROWS + i * 48 + j * 8) for j in range(6)]
+            first, last = end_derivatives(values)
+            face1[0, v * 6 + i] = values[0]
+            face1[1, v * 6 + i] = values[5]
+            face1[0, (NV + v) * 6 + i] = first
+            face1[1, (NV + v) * 6 + i] = last
+        return carry
+
+    lax.fori_loop(0, 6, wall_row, 0)
+
+
+def volume_wall(field, codes, base, prims, face1, near1, face0, near0):
+    step = TIME_STEP
 
     def wall_row(i, carry):
         row = i * 48
         nodes = [[tile_at(prims, q * VROWS + row + j * 8) for q in range(6)] for j in range(6)]
         sums = line_fluxes(nodes, 1)
-        lines = [[tile_at(field, v * VROWS + row + j * 8) for j in range(6)] for v in range(NV)]
-        ends = [end_derivatives(line) for line in lines]
-        low = ([line[0] for line in lines], [end[0] for end in ends], [], [])
-        high = ([line[5] for line in lines], [end[1] for end in ends], [], [])
-        for v in range(NV):
-            sign = -1.0 if 1 <= v <= 3 else 1.0
-            low[2].append(jnp.where(low_wall, sign * low[0][v], take_lanes(high[0][v], low_index)))
-            low[3].append(jnp.where(low_wall, low[1][v], take_lanes(high[1][v], low_index)))
-            high[2].append(jnp.where(high_wall, sign * high[0][v], take_lanes(low[0][v], high_index)))
-            high[3].append(jnp.where(high_wall, high[1][v], take_lanes(low[1][v], high_index)))
+        low, high = sides(codes, 2, face1, near1, 6, i)
         terms = face_terms(low, high, 1)
         for v in range(NV):
-            second = second_derivative(lines[v], step * VISCOSITY)
+            line = [tile_at(field, v * VROWS + row + j * 8) for j in range(6)]
+            second = second_derivative(line, step * VISCOSITY)
             values = [second[j] - float(step / WEIGHTS[j]) * sums[j][v] for j in range(6)]
             values = add_faces(values, terms, v, step)
             for j in range(6):
                 where = v * VROWS + row + j * 8
                 put_tile(base, where, tile_at(base, where) + values[j])
+        take_local(codes, 0, face0, near0, 6, i)
         return carry
 
     lax.fori_loop(0, 6, wall_row, 0)
+
+
+def volume_span(field, codes, base, prims, face2, near2):
+    step = TIME_STEP
 
     def span_row(chunk, carry):
         nodes = [[line_at(prims, q, chunk, k) for q in range(6)] for k in range(6)]
@@ -329,71 +381,53 @@
             for k in range(6):
                 value = second[k] - float(step / WEIGHTS[k]) * sums[k][v]
                 put_line(base, v, chunk, k, line_at(base, v, chunk, k) + value)
+        take_local(codes, 4, face2, near2, 5, chunk)
         return carry
 
     lax.fori_loop(0, 5, span_row, 0)
 
-    for face, near, tiles, first_side in ((face0, near0, 6, 0), (face2, near2, 5, 4)):
-        for side in range(2):
-            code = codes[first_side + side]
-            index, wall = code & 127, code >= WALL
-
-            def local(t, carry, face=face, near=near, tiles=tiles, side=side, index=index, wall=wall):
-                for q in range(2 * NV):
-                    sign = -1.0 if 1 <= q <= 3 else 1.0
-                    own = face[side, q * tiles + t]
-                    near[side, q * tiles + t] = jnp.where(
-                        wall, sign * own, take_lanes(face[1 - side, q * tiles + t], index)
-                    )
-                return carry
-
-            lax.fori_loop(0, tiles, local, 0)
-
 
 def surface_update(
-    section, last, parity, codes, field, base, face0, face2, near0, near2, received,
-    new_field, new_register, other0, other2, work,
+    section, last, codes, field, base, face0, face2, near0, near2, received,
+    new_field, new_register, got0, got2, work,
 ):
+    flow_a, flow_b, span_a, span_b = received
+    flow_odd, span_odd = lax.axis_index("px") & 1, lax.axis_index("py") & 1
+    got2[1 - span_odd] = span_a[...]
+    got2[span_odd] = span_b[pl.ds(0, 25)]
+    got0[1 - flow_odd] = flow_a[...]
+    got0[flow_odd] = flow_b[pl.ds(0, 15)]
+    surface_span(codes, base, face2, near2, got2, work)
+    surface_flow(section, last, codes, field, face0, near0, got0, new_field, new_register, work)
+
+
+def sides(codes, first_side, own, near, tiles, t, got=None, groups=1):
+    result = []
+    for side in range(2):
+        code = codes[first_side + side]
+        wall = code >= WALL
+        received = (code & RECEIVED) != 0
+        own_values, other_values = [], []
+        for q in range(2 * NV):
+            row = q * tiles + t
+            own_value = own[side, row]
+            other_value = near[side, row]
+            if got is not None:
+                share = 2 * NV * tiles // groups
+                index = (code + (128 // groups) * (row // share)) & 127
+                other_value = jnp.where(received, take_lanes(got[side, row % share], index), other_value)
+            mirrored = -own_value if 1 <= q <= 3 else own_value
+            own_values.append(own_value)
+            other_values.append(jnp.where(wall, mirrored, other_value))
+        result.append((own_values[:NV], own_values[NV:], other_values[:NV], other_values[NV:]))
+    return result
+
+
+def surface_span(codes, base, face2, near2, got2, work):
     step = TIME_STEP
-    flow_a, flow_b, span_a, span_b = received
-    flow_odd, span_odd = parity[0], parity[1]
-    for side, got in ((1 - flow_odd, flow_a), (flow_odd, flow_b)):
-        code = codes[side]
-        index = code & 127
-        mask = (code & RECEIVED) != 0
-        for g in range(4):
-            shifted = index + 32 * g
-            shifted = shifted & 127
-            for t in range(15):
-                other0[side, 15 * g + t] = jnp.where(
-                    mask, take_lanes(got[t], shifted), near0[side, 15 * g + t]
-                )
-    for side, got in ((1 - span_odd, span_a), (span_odd, span_b)):
-        code = codes[4 + side]
-        index = code & 127
-        mask = (code & RECEIVED) != 0
-        for g in range(2):
-            shifted = (index + 64 * g) & 127
-            for t in range(25):
-                other2[side, 25 * g + t] = jnp.where(
-                    mask, take_lanes(got[t], shifted), near2[side, 25 * g + t]
-                )
-
-    def sides(own, other, tiles, t):
-        result = []
-        for side in range(2):
-            result.append(
-                (
-                    [own[side, v * tiles + t] for v in range(NV)],
-                    [own[side, (NV + v) * tiles + t] for v in range(NV)],
-                    [other[side, v * tiles + t] for v in range(NV)],
-                    [other[side, (NV + v) * tiles + t] for v in range(NV)],
-                )
-            )
-        return result
 
     def span_row(chunk, carry):
-        low, high = sides(face2, other2, 5, chunk)
+        low, high = sides(codes, 4, face2, near2, 5, chunk, got2, 2)
         terms = face_terms(low, high, 2)
         for v in range(NV):
             values = [line_at(base, v, chunk, k) for k in range(6)]
@@ -402,10 +436,15 @@
                 put_line(work, v, chunk, k, values[k])
         return carry
 
-    lax.fori_loop(0, 5, span_row, 0)
+    for chunk in range(5):
+        span_row(chunk, 0)
+
+
+def surface_flow(section, last, codes, field, face0, near0, got0, new_field, new_register, work):
+    step = TIME_STEP
 
     def flow_row(j, carry):
-        low, high = sides(face0, other0, 6, j)
+        low, high = sides(codes, 0, face0, near0, 6, j, got0, 4)
         terms = face_terms(low, high, 0)
         for v in range(NV):
             rows = [v * VROWS + i * 48 + j * 8 for i in range(6)]
@@ -420,29 +459,30 @@
                     put_tile(new_register, rows[i], values[i])
         return carry
 
-    lax.fori_loop(0, 6, flow_row, 0)
+    for j in range(6):
+        flow_row(j, 0)
 
 
 def surface_kernel(
-    section, parity, codes, field, base, face0, face2, near0, near2, ra, rb, rc, rd,
+    section, codes, field, base, face0, face2, near0, near2, ra, rb, rc, rd,
     new_field, new_register, new_face0, new_face2, flow_a, flow_b, span_a, span_b,
-    other0, other2, work,
+    got0, got2, work,
 ):
     surface_update(
-        section, False, parity, codes, field, base, face0, face2, near0, near2, (ra, rb, rc, rd),
-        new_field, new_register, other0, other2, work,
+        section, False, codes, field, base, face0, face2, near0, near2, (ra, rb, rc, rd),
+        new_field, new_register, got0, got2, work,
     )
     make_faces(new_field, new_face0, new_face2)
-    pack_faces(parity, codes, new_face0, new_face2, flow_a, flow_b, span_a, span_b)
+    pack_faces(codes, new_face0, new_face2, flow_a, flow_b, span_a, span_b)
 
 
 def last_kernel(
-    section, parity, codes, field, base, face0, face2, near0, near2, ra, rb, rc, rd,
-    advanced, register, other0, other2, work,
+    section, codes, field, base, face0, face2, near0, near2, ra, rb, rc, rd,
+    advanced, register, got0, got2, work,
 ):
     surface_update(
-        section, True, parity, codes, field, base, face0, face2, near0, near2, (ra, rb, rc, rd),
-        advanced, register, other0, other2, work,
+        section, True, codes, field, base, face0, face2, near0, near2, (ra, rb, rc, rd),
+        advanced, register, got0, got2, work,
     )
 
 
@@ -451,7 +491,6 @@
 
 
 VMEM_SPEC = pl.BlockSpec(memory_space=pltpu.VMEM)
-SMEM_SPEC = pl.BlockSpec(memory_space=pltpu.SMEM)
 PARAMS = pltpu.CompilerParams(vmem_limit_bytes=32 * 1024 * 1024)
 
 
@@ -461,26 +500,32 @@
 
 def face_outs():
     return [
-        vmem_out(FACE0), vmem_out(FACE2), vmem_out(FLOW_PACK), vmem_out(FLOW_PACK),
-        vmem_out(SPAN_PACK), vmem_out(SPAN_PACK),
+        vmem_out(FACE0), vmem_out(FACE2), vmem_out(FLOW_PACK), vmem_out(FLOW_FAR),
+        vmem_out(SPAN_PACK), vmem_out(SPAN_FAR),
     ]
 
 
-def first_call(parity, conserved, lists):
+def first_call(*args):
     outs = [vmem_out(FIELD), vmem_out(CODES, jnp.int32)] + face_outs()
     return pl.pallas_call(
         first_kernel,
         out_shape=outs,
-        in_specs=[SMEM_SPEC, VMEM_SPEC, VMEM_SPEC],
+        in_specs=[pl.BlockSpec(memory_space=pltpu.HBM)] * len(args),
         out_specs=[VMEM_SPEC] * len(outs),
+        scratch_shapes=[
+            pltpu.VMEM((NV, 6, 6, 6, 128), jnp.float32),
+            pltpu.VMEM((1, 2, 32), jnp.int32),
+            pltpu.VMEM((1, 2, 64), jnp.int32),
+            pltpu.VMEM((6, 128), jnp.int32),
+            pltpu.SemaphoreType.DMA((3,)),
+            pltpu.SemaphoreType.DMA((NV,)),
+        ],
         compiler_params=PARAMS,
         name="first_faces",
-    )(parity, conserved, lists)
+    )(*[pltpu.with_memory_space_constraint(value, pltpu.HBM) for value in args])
 
 
 def volume_call(section, field, register, codes, face0, face2):
-    outs = [vmem_out(FIELD), vmem_out(FACE0), vmem_out(FACE2)]
-
     def kernel(*refs):
         if section > 0:
             volume_kernel(section, *refs)
@@ -488,19 +533,24 @@
             volume_kernel(section, refs[0], None, *refs[1:])
 
     args = [field, codes, face0, face2] if section == 0 else [field, register, codes, face0, face2]
+    outs = [vmem_out(FIELD), vmem_out(FACE0), vmem_out(FACE2)]
     return pl.pallas_call(
         kernel,
         out_shape=outs,
         in_specs=[VMEM_SPEC] * len(args),
         out_specs=[VMEM_SPEC] * len(outs),
-        scratch_shapes=[pltpu.VMEM((6 * VROWS, 128), jnp.float32)],
+        scratch_shapes=[
+            pltpu.VMEM((6 * VROWS, 128), jnp.float32),
+            pltpu.VMEM(FACE0, jnp.float32),
+            pltpu.VMEM(FACE0, jnp.float32),
+        ],
         compiler_params=PARAMS,
         cost_estimate=pl.CostEstimate(flops=10**7, bytes_accessed=4 * 10**6, transcendentals=0),
         name="volume",
     )(*map(in_vmem, args))
 
 
-def surface_call(section, parity, *args):
+def surface_call(section, *args):
     last = section == len(RK_A) - 1
 
     def kernel(*refs):
@@ -513,16 +563,16 @@
     return pl.pallas_call(
         kernel,
         out_shape=outs,
-        in_specs=[SMEM_SPEC] + [VMEM_SPEC] * len(args),
+        in_specs=[VMEM_SPEC] * len(args),
         out_specs=[VMEM_SPEC] * len(outs),
         scratch_shapes=[
-            pltpu.VMEM(FACE0, jnp.float32),
-            pltpu.VMEM(FACE2, jnp.float32),
+            pltpu.VMEM((2,) + FLOW_PACK, jnp.float32),
+            pltpu.VMEM((2,) + SPAN_PACK, jnp.float32),
             pltpu.VMEM(FIELD, jnp.float32),
         ],
         compiler_params=PARAMS,
         name="surface",
-    )(parity, *map(in_vmem, args))
+    )(*map(in_vmem, args))
 
 
 def swap(value, axis, crossing):
@@ -535,25 +585,21 @@
 
 
 def body(conserved, flow_lists, span_lists, face_source):
-    parity = jnp.stack([lax.axis_index("px") & 1, lax.axis_index("py") & 1]).astype(jnp.int32)
-    lists = jnp.concatenate(
-        [face_source, jnp.tile(flow_lists[0], (1, 4)), jnp.tile(span_lists[0], (1, 2))], axis=0
-    )
-    field, codes, face0, face2, *packs = first_call(parity, conserved, lists)
+    field, codes, *faces = first_call(conserved, flow_lists, span_lists, face_source)
     register = None
     for section in range(len(RK_A)):
-        flow_a, flow_b, span_a, span_b = packs
+        face0, face2, flow_a, flow_b, span_a, span_b = faces
         rd = swap(span_b, "py", True)
         rc = swap(span_a, "py", False)
         rb = swap(flow_b, "px", True)
         ra = swap(flow_a, "px", False)
         base, near0, near2 = volume_call(section, field, register, codes, face0, face2)
         outs = surface_call(
-            section, parity, codes, field, base, face0, face2, near0, near2, ra, rb, rc, rd
+            section, codes, field, base, face0, face2, near0, near2, ra, rb, rc, rd
         )
         if section == len(RK_A) - 1:
             return tuple(outs)
-        field, register, face0, face2, *packs = outs
+        field, register, *faces = outs
 
 
 def solution(mesh):

time: 65.5 us -> 54.9 us (0.84)
  Pallas kernels: 33.6 us -> 22.5 us
  starting transfers between devices: 27.5 us -> 31 us
  local copies, waits for them, and re-layouts: 3.25 us -> 0 us
    pallas_call x5, Pallas kernels: 20.9 us -> 12.8 us  [volume_call(): pl.pallas_call(kernel, out_shape=outs, in_specs=[VMEM_SPEC] * len(args),...]
    ppermute x20, starting transfers between devices: 27.5 us -> 31 us  [swap(): return lax.ppermute(value, axis, pairs)]
    unnamed x8 -> x0, local copies, waits for them, and re-layouts: 3.08 us -> none
    pallas_call x6, Pallas kernels: 12.7 us -> 9.73 us  [the longest x5 7.91 us: surface_call(): pl.pallas_call(kernel, out_shape=outs, in_specs=[VMEM_SPEC] * len(args),...]
  transfers between devices with their start and end apart: 20 -> 20, of which waited for: 0 -> 1; matrix products, arithmetic and copies ran while one was open for 0% -> 0% of each run, Pallas kernels for 32% -> 23%
where the time goes in v1:
time: 54.9 us; the launch traced here: 54.6 us
  starting transfers between devices  31 us (56%)
  Pallas kernels  22.5 us (41%)
  between operations  0.85 us (2%)
    ppermute x20, starting transfers between devices, swap(): return lax.ppermute(value, axis, pairs)  31 us
    pallas_call x5, Pallas kernels, volume_call(): pl.pallas_call(kernel, out_shape=outs, in_specs=[VMEM_SPEC] * len(args),...  12.8 us
    pallas_call x5, Pallas kernels, surface_call(): pl.pallas_call(kernel, out_shape=outs, in_specs=[VMEM_SPEC] * len(args),...  7.91 us
    pallas_call x1, Pallas kernels, first_call(): pl.pallas_call(first_kernel, out_shape=outs, in_specs=[pl.BlockSpec(memor...  1.82 us
  transfers between devices with their start and end apart: 20, of which 1 were waited for; matrix products, arithmetic and copies ran while one was open for 0% of the time, Pallas kernels for 23%

profile of v1, /device:TPU:1, one launch (start us, length us, event | category | flops | bytes accessed | tf_op | source)
XLA Modules:
  0.0 54.6 jit_solution(10932944316988426940)
XLA Ops:
  0.6 1.8 %first_faces.1 = (f32[1600,128]{1,0:T(8,128)S(1)}, s32[10,8,128]{2,1,0:T(8,128)S(1)}, f32[2,60,8,128]{3,2,1,0:T(8,128)S(1)}, f32[2,50,8,128]{3,2,1,0:T(8,128)S(1...) custom-call(f32[5,6,6,6,128]{4,3,2,1,0:T(8,128)} %conserved.1, ...), custom_call_target="tpu_custom_call" | custom-call | tf_op jit(solution)/shard_map/first_faces/pallas_call | solution.py:510
  2.5 7.1 %collective-permute-start.3 = (f32[26,8,128]{2,1,0:T(8,128)S(1)}, f32[26,8,128]{2,1,0:T(8,128)S(1)}, u32[]{:S(2)}, u32[]{:S(2)}) collective-permute-start(f32[26,8,128]{2,1,0:T(8,128)S(1)} %get-tuple-element.67), channel_id=1, source_target_pairs={{0,15},{1,2},{2,1},{3,4},{4,3},{5,6},{6,5},{7,8},{8,7},{9,10},{10,... | collective-permute-start | bytes 319496 | tf_op jit(solution)/shard_map/ppermute | solution.py:584
  9.6 2.1 %collective-permute-start.1 = (f32[16,8,128]{2,1,0:T(8,128)S(1)}, f32[16,8,128]{2,1,0:T(8,128)S(1)}, u32[]{:S(2)}, u32[]{:S(2)}) collective-permute-start(f32[16,8,128]{2,1,0:T(8,128)S(1)} %get-tuple-element.65), channel_id=1, source_target_pairs={{0,112},{16,32},{32,16},{48,64},{64,48},{80,96},{96,80},{112,0},{1... | collective-permute-start | bytes 196616 | tf_op jit(solution)/shard_map/ppermute | solution.py:584
  11.6 0.8 %collective-permute-start = (f32[15,8,128]{2,1,0:T(8,128)S(1)}, f32[15,8,128]{2,1,0:T(8,128)S(1)}, u32[]{:S(2)}, u32[]{:S(2)}) collective-permute-start(f32[15,8,128]{2,1,0:T(8,128)S(1)} %get-tuple-element.64), channel_id=1, source_target_pairs={{0,16},{16,0},{32,48},{48,32},{64,80},{80,64},{96,112},{112,96},{1... | collective-permute-start | bytes 184328 | tf_op jit(solution)/shard_map/ppermute | solution.py:584
  12.5 2.5 %volume.5 = (f32[1600,128]{1,0:T(8,128)S(1)}, f32[2,60,8,128]{3,2,1,0:T(8,128)S(1)}, f32[2,50,8,128]{3,2,1,0:T(8,128)S(1)}) custom-call(f32[1600,128]{1,0:T(8,128)S(1)} %get-tuple-element.58.refs_0_.refs_1_, s32[10,8,128]{2,1,0:T(8,128)S(1)} %get-tuple-element.57.refs_1_.refs_0_.refs_2_, f32[2,60,8,128]{3,2,1,0:T(8,128)S(1)} %get-tuple-element.59.refs_2_.refs_3_, ...), custom_call_target="tpu_custom_call" | custom-call | flops 10000000 | bytes 4000000 | tf_op jit(solution)/shard_map/volume/pallas_call | solution.py:537
  15.0 1.5 %surface.5 = (f32[1600,128]{1,0:T(8,128)S(1)}, f32[1600,128]{1,0:T(8,128)S(1)}, f32[2,60,8,128]{3,2,1,0:T(8,128)S(1)}, f32[2,50,8,128]{3,2,1,0:T(8,128)S(1)}, f3...) custom-call(s32[10,8,128]{2,1,0:T(8,128)S(1)} %get-tuple-element.57., ...), custom_call_target="tpu_custom_call" | custom-call | tf_op jit(solution)/shard_map/surface/pallas_call | solution.py:563
  16.5 1.5 %collective-permute-start.7 = (f32[26,8,128]{2,1,0:T(8,128)S(1)}, f32[26,8,128]{2,1,0:T(8,128)S(1)}, u32[]{:S(2)}, u32[]{:S(2)}) collective-permute-start(f32[26,8,128]{2,1,0:T(8,128)S(1)} %get-tuple-element.78), channel_id=1, source_target_pairs={{0,15},{1,2},{2,1},{3,4},{4,3},{5,6},{6,5},{7,8},{8,7},{9,10},{10,... | collective-permute-start | bytes 319496 | tf_op jit(solution)/shard_map/ppermute | solution.py:584
  18.0 0.1 collective-permute-start.6
  18.2 3.1 %collective-permute-start.5 = (f32[16,8,128]{2,1,0:T(8,128)S(1)}, f32[16,8,128]{2,1,0:T(8,128)S(1)}, u32[]{:S(2)}, u32[]{:S(2)}) collective-permute-start(f32[16,8,128]{2,1,0:T(8,128)S(1)} %get-tuple-element.76), channel_id=1, source_target_pairs={{0,112},{16,32},{32,16},{48,64},{64,48},{80,96},{96,80},{112,0},{1... | collective-permute-start | bytes 196616 | tf_op jit(solution)/shard_map/ppermute | solution.py:584
  21.2 2.6 %volume.6 = (f32[1600,128]{1,0:T(8,128)S(1)}, f32[2,60,8,128]{3,2,1,0:T(8,128)S(1)}, f32[2,50,8,128]{3,2,1,0:T(8,128)S(1)}) custom-call(f32[1600,128]{1,0:T(8,128)S(1)} %get-tuple-element.68.refs_0_.refs_1_, f32[1600,128]{1,0:T(8,128)S(1)} %get-tuple-element.69.refs_1_, s32[10,8,128]{2,1,0:T(8,128)S(1)} %get-tuple-element.57.refs_1_.refs_0_.refs_2_, ...), custom_call_target="tpu_custom_call" | custom-call | flops 10000000 | bytes 4000000 | tf_op jit(solution)/shard_map/volume/pallas_call | solution.py:537
  23.8 0.2 collective-permute-done.7.refs_10_
  24.1 1.5 %surface.6 = (f32[1600,128]{1,0:T(8,128)S(1)}, f32[1600,128]{1,0:T(8,128)S(1)}, f32[2,60,8,128]{3,2,1,0:T(8,128)S(1)}, f32[2,50,8,128]{3,2,1,0:T(8,128)S(1)}, f3...) custom-call(s32[10,8,128]{2,1,0:T(8,128)S(1)} %get-tuple-element.57., ...), custom_call_target="tpu_custom_call" | custom-call | tf_op jit(solution)/shard_map/surface/pallas_call | solution.py:563
  25.5 2.4 %collective-permute-start.11 = (f32[26,8,128]{2,1,0:T(8,128)S(1)}, f32[26,8,128]{2,1,0:T(8,128)S(1)}, u32[]{:S(2)}, u32[]{:S(2)}) collective-permute-start(f32[26,8,128]{2,1,0:T(8,128)S(1)} %get-tuple-element.89), channel_id=1, source_target_pairs={{0,15},{1,2},{2,1},{3,4},{4,3},{5,6},{6,5},{7,8},{8,7},{9,10},{10,... | collective-permute-start | bytes 319496 | tf_op jit(solution)/shard_map/ppermute | solution.py:584
  27.9 2.9 %collective-permute-start.9 = (f32[16,8,128]{2,1,0:T(8,128)S(1)}, f32[16,8,128]{2,1,0:T(8,128)S(1)}, u32[]{:S(2)}, u32[]{:S(2)}) collective-permute-start(f32[16,8,128]{2,1,0:T(8,128)S(1)} %get-tuple-element.87), channel_id=1, source_target_pairs={{0,112},{16,32},{32,16},{48,64},{64,48},{80,96},{96,80},{112,0},{1... | collective-permute-start | bytes 196616 | tf_op jit(solution)/shard_map/ppermute | solution.py:584
  30.8 2.6 %volume.7 = (f32[1600,128]{1,0:T(8,128)S(1)}, f32[2,60,8,128]{3,2,1,0:T(8,128)S(1)}, f32[2,50,8,128]{3,2,1,0:T(8,128)S(1)}) custom-call(f32[1600,128]{1,0:T(8,128)S(1)} %get-tuple-element.79.refs_0_.refs_1_, f32[1600,128]{1,0:T(8,128)S(1)} %get-tuple-element.80.refs_1_, s32[10,8,128]{2,1,0:T(8,128)S(1)} %get-tuple-element.57.refs_1_.refs_0_.refs_2_, ...), custom_call_target="tpu_custom_call" | custom-call | flops 10000000 | bytes 4000000 | tf_op jit(solution)/shard_map/volume/pallas_call | solution.py:537
  33.4 1.5 %surface.7 = (f32[1600,128]{1,0:T(8,128)S(1)}, f32[1600,128]{1,0:T(8,128)S(1)}, f32[2,60,8,128]{3,2,1,0:T(8,128)S(1)}, f32[2,50,8,128]{3,2,1,0:T(8,128)S(1)}, f3...) custom-call(s32[10,8,128]{2,1,0:T(8,128)S(1)} %get-tuple-element.57., ...), custom_call_target="tpu_custom_call" | custom-call | tf_op jit(solution)/shard_map/surface/pallas_call | solution.py:563
  34.9 1.8 %collective-permute-start.15 = (f32[26,8,128]{2,1,0:T(8,128)S(1)}, f32[26,8,128]{2,1,0:T(8,128)S(1)}, u32[]{:S(2)}, u32[]{:S(2)}) collective-permute-start(f32[26,8,128]{2,1,0:T(8,128)S(1)} %get-tuple-element.100), channel_id=1, source_target_pairs={{0,15},{1,2},{2,1},{3,4},{4,3},{5,6},{6,5},{7,8},{8,7},{9,10},{10,... | collective-permute-start | bytes 319496 | tf_op jit(solution)/shard_map/ppermute | solution.py:584
  36.8 3.6 %collective-permute-start.13 = (f32[16,8,128]{2,1,0:T(8,128)S(1)}, f32[16,8,128]{2,1,0:T(8,128)S(1)}, u32[]{:S(2)}, u32[]{:S(2)}) collective-permute-start(f32[16,8,128]{2,1,0:T(8,128)S(1)} %get-tuple-element.98), channel_id=1, source_target_pairs={{0,112},{16,32},{32,16},{48,64},{64,48},{80,96},{96,80},{112,0},{1... | collective-permute-start | bytes 196616 | tf_op jit(solution)/shard_map/ppermute | solution.py:584
  40.4 2.6 %volume.8 = (f32[1600,128]{1,0:T(8,128)S(1)}, f32[2,60,8,128]{3,2,1,0:T(8,128)S(1)}, f32[2,50,8,128]{3,2,1,0:T(8,128)S(1)}) custom-call(f32[1600,128]{1,0:T(8,128)S(1)} %get-tuple-element.90.refs_0_.refs_1_, f32[1600,128]{1,0:T(8,128)S(1)} %get-tuple-element.91.refs_1_, s32[10,8,128]{2,1,0:T(8,128)S(1)} %get-tuple-element.57.refs_1_.refs_0_.refs_2_, ...), custom_call_target="tpu_custom_call" | custom-call | flops 10000000 | bytes 4000000 | tf_op jit(solution)/shard_map/volume/pallas_call | solution.py:537
  43.0 1.5 %surface.8 = (f32[1600,128]{1,0:T(8,128)S(1)}, f32[1600,128]{1,0:T(8,128)S(1)}, f32[2,60,8,128]{3,2,1,0:T(8,128)S(1)}, f32[2,50,8,128]{3,2,1,0:T(8,128)S(1)}, f3...) custom-call(s32[10,8,128]{2,1,0:T(8,128)S(1)} %get-tuple-element.57., ...), custom_call_target="tpu_custom_call" | custom-call | tf_op jit(solution)/shard_map/surface/pallas_call | solution.py:563
  44.5 1.8 %collective-permute-start.19 = (f32[26,8,128]{2,1,0:T(8,128)S(1)}, f32[26,8,128]{2,1,0:T(8,128)S(1)}, u32[]{:S(2)}, u32[]{:S(2)}) collective-permute-start(f32[26,8,128]{2,1,0:T(8,128)S(1)} %get-tuple-element.111), channel_id=1, source_target_pairs={{0,15},{1,2},{2,1},{3,4},{4,3},{5,6},{6,5},{7,8},{8,7},{9,10},{10,... | collective-permute-start | bytes 319496 | tf_op jit(solution)/shard_map/ppermute | solution.py:584
  46.4 3.6 %collective-permute-start.17 = (f32[16,8,128]{2,1,0:T(8,128)S(1)}, f32[16,8,128]{2,1,0:T(8,128)S(1)}, u32[]{:S(2)}, u32[]{:S(2)}) collective-permute-start(f32[16,8,128]{2,1,0:T(8,128)S(1)} %get-tuple-element.109), channel_id=1, source_target_pairs={{0,112},{16,32},{32,16},{48,64},{64,48},{80,96},{96,80},{112,0},{1... | collective-permute-start | bytes 196616 | tf_op jit(solution)/shard_map/ppermute | solution.py:584
  50.0 2.6 %volume.9 = (f32[1600,128]{1,0:T(8,128)S(1)}, f32[2,60,8,128]{3,2,1,0:T(8,128)S(1)}, f32[2,50,8,128]{3,2,1,0:T(8,128)S(1)}) custom-call(f32[1600,128]{1,0:T(8,128)S(1)} %get-tuple-element.101.refs_0_.refs_1_, f32[1600,128]{1,0:T(8,128)S(1)} %get-tuple-element.102.refs_1_, s32[10,8,128]{2,1,0:T(8,128)S(1)} %get-tuple-element.57.refs_1_.refs_0_.refs_2_, ...), custom_call_target="tpu_custom_call" | custom-call | flops 10000000 | bytes 4000000 | tf_op jit(solution)/shard_map/volume/pallas_call | solution.py:537
  52.6 2.0 %surface.9 = (f32[5,6,6,6,128]{4,3,2,1,0:T(8,128)}, f32[5,6,6,6,128]{4,3,2,1,0:T(8,128)}) custom-call(s32[10,8,128]{2,1,0:T(8,128)S(1)} %get-tuple-element.57.refs_1_.refs_0_.refs_2_, f32[1600,128]{1,0:T(8,128)S(1)} %get-tuple-element.101.refs_0_.refs_1_, f32[1600,128]{1,0:T(8,128)S(1)} %get-tuple-element.105.refs_2_, ...), custom_call_target="tpu_custom_call" | custom-call | tf_op jit(solution)/shard_map/surface/pallas_call | solution.py:563
  (27 shorter events, 0.3 us)
Async XLA Ops:
  2.5 12.6 %collective-permute-start.3 = (f32[26,8,128]{2,1,0:T(8,128)S(1)}, f32[26,8,128]{2,1,0:T(8,128)S(1)}, u32[]{:S(2)}, u32[]{:S(2)}) collective-permute-start(f32[26,8,128]{2,1,0:T(8,128)S(1)} %get-tuple-element.67), channel_id=1, source_target_pairs={{0,15},{1,2},{2,1},{3,4},{4,3},{5,6},{6,5},{7,8},{8,7},{9,10},{10,... | collective-permute-start | bytes 319496 | tf_op jit(solution)/shard_map/ppermute | solution.py:584
  9.6 5.4 %collective-permute-start.2 = (f32[25,8,128]{2,1,0:T(8,128)S(1)}, f32[25,8,128]{2,1,0:T(8,128)S(1)}, u32[]{:S(2)}, u32[]{:S(2)}) collective-permute-start(f32[25,8,128]{2,1,0:T(8,128)S(1)} %get-tuple-element.66), channel_id=1, source_target_pairs={{0,1},{1,0},{2,3},{3,2},{4,5},{5,4},{6,7},{7,6},{8,9},{9,8},{10,11... | collective-permute-start | bytes 307208 | tf_op jit(solution)/shard_map/ppermute | solution.py:584
  9.6 5.4 %collective-permute-start.1 = (f32[16,8,128]{2,1,0:T(8,128)S(1)}, f32[16,8,128]{2,1,0:T(8,128)S(1)}, u32[]{:S(2)}, u32[]{:S(2)}) collective-permute-start(f32[16,8,128]{2,1,0:T(8,128)S(1)} %get-tuple-element.65), channel_id=1, source_target_pairs={{0,112},{16,32},{32,16},{48,64},{64,48},{80,96},{96,80},{112,0},{1... | collective-permute-start | bytes 196616 | tf_op jit(solution)/shard_map/ppermute | solution.py:584
  11.6 3.4 %collective-permute-start = (f32[15,8,128]{2,1,0:T(8,128)S(1)}, f32[15,8,128]{2,1,0:T(8,128)S(1)}, u32[]{:S(2)}, u32[]{:S(2)}) collective-permute-start(f32[15,8,128]{2,1,0:T(8,128)S(1)} %get-tuple-element.64), channel_id=1, source_target_pairs={{0,16},{16,0},{32,48},{48,32},{64,80},{80,64},{96,112},{112,96},{1... | collective-permute-start | bytes 184328 | tf_op jit(solution)/shard_map/ppermute | solution.py:584
  16.5 7.5 %collective-permute-start.7 = (f32[26,8,128]{2,1,0:T(8,128)S(1)}, f32[26,8,128]{2,1,0:T(8,128)S(1)}, u32[]{:S(2)}, u32[]{:S(2)}) collective-permute-start(f32[26,8,128]{2,1,0:T(8,128)S(1)} %get-tuple-element.78), channel_id=1, source_target_pairs={{0,15},{1,2},{2,1},{3,4},{4,3},{5,6},{6,5},{7,8},{8,7},{9,10},{10,... | collective-permute-start | bytes 319496 | tf_op jit(solution)/shard_map/ppermute | solution.py:584
  18.0 5.8 %collective-permute-start.6 = (f32[25,8,128]{2,1,0:T(8,128)S(1)}, f32[25,8,128]{2,1,0:T(8,128)S(1)}, u32[]{:S(2)}, u32[]{:S(2)}) collective-permute-start(f32[25,8,128]{2,1,0:T(8,128)S(1)} %get-tuple-element.77), channel_id=1, source_target_pairs={{0,1},{1,0},{2,3},{3,2},{4,5},{5,4},{6,7},{7,6},{8,9},{9,8},{10,11... | collective-permute-start | bytes 307208 | tf_op jit(solution)/shard_map/ppermute | solution.py:584
  18.2 5.7 %collective-permute-start.5 = (f32[16,8,128]{2,1,0:T(8,128)S(1)}, f32[16,8,128]{2,1,0:T(8,128)S(1)}, u32[]{:S(2)}, u32[]{:S(2)}) collective-permute-start(f32[16,8,128]{2,1,0:T(8,128)S(1)} %get-tuple-element.76), channel_id=1, source_target_pairs={{0,112},{16,32},{32,16},{48,64},{64,48},{80,96},{96,80},{112,0},{1... | collective-permute-start | bytes 196616 | tf_op jit(solution)/shard_map/ppermute | solution.py:584
  21.2 2.6 %collective-permute-start.4 = (f32[15,8,128]{2,1,0:T(8,128)S(1)}, f32[15,8,128]{2,1,0:T(8,128)S(1)}, u32[]{:S(2)}, u32[]{:S(2)}) collective-permute-start(f32[15,8,128]{2,1,0:T(8,128)S(1)} %get-tuple-element.75), channel_id=1, source_target_pairs={{0,16},{16,0},{32,48},{48,32},{64,80},{80,64},{96,112},{112,96},{1... | collective-permute-start | bytes 184328 | tf_op jit(solution)/shard_map/ppermute | solution.py:584
  25.5 7.9 %collective-permute-start.11 = (f32[26,8,128]{2,1,0:T(8,128)S(1)}, f32[26,8,128]{2,1,0:T(8,128)S(1)}, u32[]{:S(2)}, u32[]{:S(2)}) collective-permute-start(f32[26,8,128]{2,1,0:T(8,128)S(1)} %get-tuple-element.89), channel_id=1, source_target_pairs={{0,15},{1,2},{2,1},{3,4},{4,3},{5,6},{6,5},{7,8},{8,7},{9,10},{10,... | collective-permute-start | bytes 319496 | tf_op jit(solution)/shard_map/ppermute | solution.py:584
  27.9 5.5 %collective-permute-start.10 = (f32[25,8,128]{2,1,0:T(8,128)S(1)}, f32[25,8,128]{2,1,0:T(8,128)S(1)}, u32[]{:S(2)}, u32[]{:S(2)}) collective-permute-start(f32[25,8,128]{2,1,0:T(8,128)S(1)} %get-tuple-element.88), channel_id=1, source_target_pairs={{0,1},{1,0},{2,3},{3,2},{4,5},{5,4},{6,7},{7,6},{8,9},{9,8},{10,11... | collective-permute-start | bytes 307208 | tf_op jit(solution)/shard_map/ppermute | solution.py:584
  27.9 5.5 %collective-permute-start.9 = (f32[16,8,128]{2,1,0:T(8,128)S(1)}, f32[16,8,128]{2,1,0:T(8,128)S(1)}, u32[]{:S(2)}, u32[]{:S(2)}) collective-permute-start(f32[16,8,128]{2,1,0:T(8,128)S(1)} %get-tuple-element.87), channel_id=1, source_target_pairs={{0,112},{16,32},{32,16},{48,64},{64,48},{80,96},{96,80},{112,0},{1... | collective-permute-start | bytes 196616 | tf_op jit(solution)/shard_map/ppermute | solution.py:584
  30.8 2.6 %collective-permute-start.8 = (f32[15,8,128]{2,1,0:T(8,128)S(1)}, f32[15,8,128]{2,1,0:T(8,128)S(1)}, u32[]{:S(2)}, u32[]{:S(2)}) collective-permute-start(f32[15,8,128]{2,1,0:T(8,128)S(1)} %get-tuple-element.86), channel_id=1, source_target_pairs={{0,16},{16,0},{32,48},{48,32},{64,80},{80,64},{96,112},{112,96},{1... | collective-permute-start | bytes 184328 | tf_op jit(solution)/shard_map/ppermute | solution.py:584
  34.9 8.1 %collective-permute-start.15 = (f32[26,8,128]{2,1,0:T(8,128)S(1)}, f32[26,8,128]{2,1,0:T(8,128)S(1)}, u32[]{:S(2)}, u32[]{:S(2)}) collective-permute-start(f32[26,8,128]{2,1,0:T(8,128)S(1)} %get-tuple-element.100), channel_id=1, source_target_pairs={{0,15},{1,2},{2,1},{3,4},{4,3},{5,6},{6,5},{7,8},{8,7},{9,10},{10,... | collective-permute-start | bytes 319496 | tf_op jit(solution)/shard_map/ppermute | solution.py:584
  36.7 6.3 %collective-permute-start.14 = (f32[25,8,128]{2,1,0:T(8,128)S(1)}, f32[25,8,128]{2,1,0:T(8,128)S(1)}, u32[]{:S(2)}, u32[]{:S(2)}) collective-permute-start(f32[25,8,128]{2,1,0:T(8,128)S(1)} %get-tuple-element.99), channel_id=1, source_target_pairs={{0,1},{1,0},{2,3},{3,2},{4,5},{5,4},{6,7},{7,6},{8,9},{9,8},{10,11... | collective-permute-start | bytes 307208 | tf_op jit(solution)/shard_map/ppermute | solution.py:584
  36.8 6.2 %collective-permute-start.13 = (f32[16,8,128]{2,1,0:T(8,128)S(1)}, f32[16,8,128]{2,1,0:T(8,128)S(1)}, u32[]{:S(2)}, u32[]{:S(2)}) collective-permute-start(f32[16,8,128]{2,1,0:T(8,128)S(1)} %get-tuple-element.98), channel_id=1, source_target_pairs={{0,112},{16,32},{32,16},{48,64},{64,48},{80,96},{96,80},{112,0},{1... | collective-permute-start | bytes 196616 | tf_op jit(solution)/shard_map/ppermute | solution.py:584
  40.4 2.6 %collective-permute-start.12 = (f32[15,8,128]{2,1,0:T(8,128)S(1)}, f32[15,8,128]{2,1,0:T(8,128)S(1)}, u32[]{:S(2)}, u32[]{:S(2)}) collective-permute-start(f32[15,8,128]{2,1,0:T(8,128)S(1)} %get-tuple-element.97), channel_id=1, source_target_pairs={{0,16},{16,0},{32,48},{48,32},{64,80},{80,64},{96,112},{112,96},{1... | collective-permute-start | bytes 184328 | tf_op jit(solution)/shard_map/ppermute | solution.py:584
  44.5 8.1 %collective-permute-start.19 = (f32[26,8,128]{2,1,0:T(8,128)S(1)}, f32[26,8,128]{2,1,0:T(8,128)S(1)}, u32[]{:S(2)}, u32[]{:S(2)}) collective-permute-start(f32[26,8,128]{2,1,0:T(8,128)S(1)} %get-tuple-element.111), channel_id=1, source_target_pairs={{0,15},{1,2},{2,1},{3,4},{4,3},{5,6},{6,5},{7,8},{8,7},{9,10},{10,... | collective-permute-start | bytes 319496 | tf_op jit(solution)/shard_map/ppermute | solution.py:584
  46.3 6.3 %collective-permute-start.18 = (f32[25,8,128]{2,1,0:T(8,128)S(1)}, f32[25,8,128]{2,1,0:T(8,128)S(1)}, u32[]{:S(2)}, u32[]{:S(2)}) collective-permute-start(f32[25,8,128]{2,1,0:T(8,128)S(1)} %get-tuple-element.110), channel_id=1, source_target_pairs={{0,1},{1,0},{2,3},{3,2},{4,5},{5,4},{6,7},{7,6},{8,9},{9,8},{10,11... | collective-permute-start | bytes 307208 | tf_op jit(solution)/shard_map/ppermute | solution.py:584
  46.4 6.2 %collective-permute-start.17 = (f32[16,8,128]{2,1,0:T(8,128)S(1)}, f32[16,8,128]{2,1,0:T(8,128)S(1)}, u32[]{:S(2)}, u32[]{:S(2)}) collective-permute-start(f32[16,8,128]{2,1,0:T(8,128)S(1)} %get-tuple-element.109), channel_id=1, source_target_pairs={{0,112},{16,32},{32,16},{48,64},{64,48},{80,96},{96,80},{112,0},{1... | collective-permute-start | bytes 196616 | tf_op jit(solution)/shard_map/ppermute | solution.py:584
  50.0 2.6 %collective-permute-start.16 = (f32[15,8,128]{2,1,0:T(8,128)S(1)}, f32[15,8,128]{2,1,0:T(8,128)S(1)}, u32[]{:S(2)}, u32[]{:S(2)}) collective-permute-start(f32[15,8,128]{2,1,0:T(8,128)S(1)} %get-tuple-element.108), channel_id=1, source_target_pairs={{0,16},{16,0},{32,48},{48,32},{64,80},{80,64},{96,112},{112,96},{1... | collective-permute-start | bytes 184328 | tf_op jit(solution)/shard_map/ppermute | solution.py:584

commit v2 on v1

--- a/solution.py
+++ b/solution.py
@@ -75,6 +75,18 @@
     ref[pl.ds(var * VROWS + chunk * 64 + k, 8, stride=8), :] = value
 
 
+def rows_loop(count, unroll, row):
+    def step(n, carry):
+        for u in range(unroll):
+            row(n * unroll + u, carry)
+        return carry
+
+    if unroll == count:
+        step(0, 0)
+    else:
+        lax.fori_loop(0, count // unroll, step, 0)
+
+
 def take_lanes(value, index):
     return jnp.take_along_axis(value, index, axis=1, mode="promise_in_bounds")
 
@@ -100,12 +112,21 @@
     return first + second, second - first
 
 
-def second_derivative(values, scale):
+def jump_parts(low, high):
+    total, difference = high + low, high - low
+    even = [float((DM[i, 5] + DM[5 - i, 5]) / 2) * total for i in range(3)]
+    odd = [float((DM[i, 5] - DM[5 - i, 5]) / 2) * difference for i in range(3)]
+    return even, odd
+
+
+def second_derivative(values, scale, jumps=None):
     even, odd = even_odd(values)
     result = [None] * 6
     for i in range(3):
         first = combine([scale * (DM2[i, m] + DM2[i, 5 - m]) / 2 for m in range(3)], even)
         second = combine([scale * (DM2[i, m] - DM2[i, 5 - m]) / 2 for m in range(3)], odd)
+        if jumps is not None:
+            first, second = first + jumps[0][i], second + jumps[1][i]
         result[i] = first + second
         result[5 - i] = first - second
     return result
@@ -146,7 +167,7 @@
     return sums
 
 
-def rusanov(left, right, direction):
+def rusanov(left, right, direction, scale):
     def parts(state):
         inverse = 1.0 / state[0]
         velocity = state[1 + direction] * inverse
@@ -162,33 +183,32 @@
     right_flux, right_speed = parts(right)
     speed = jnp.maximum(left_speed, right_speed)
     return [
-        0.5 * ((left_flux[n] + right_flux[n]) - speed * (right[n] - left[n])) for n in range(NV)
+        (0.5 * scale) * ((left_flux[n] + right_flux[n]) - speed * (right[n] - left[n]))
+        for n in range(NV)
     ]
 
 
 def face_terms(low, high, direction):
-    low_flux = rusanov(low[2], low[0], direction)
-    high_flux = rusanov(high[0], high[2], direction)
-    visc = 0.5 * VISCOSITY * LIFT
-    end_low, end_high, jump_low, jump_high = [], [], [], []
+    low_flux = rusanov(low[2], low[0], direction, TIME_STEP * LIFT)
+    high_flux = rusanov(high[0], high[2], direction, TIME_STEP * LIFT)
+    visc = TIME_STEP * 0.5 * VISCOSITY * LIFT
+    ends_low, ends_high, jumps = [], [], []
     for n in range(NV):
-        end_low.append(LIFT * low_flux[n] - visc * (low[3][n] - low[1][n]))
-        end_high.append(visc * (high[3][n] - high[1][n]) - LIFT * high_flux[n])
-        jump_low.append(visc * (low[2][n] - low[0][n]))
-        jump_high.append(visc * (high[2][n] - high[0][n]))
-    return end_low, end_high, jump_low, jump_high
-
-
-def add_faces(values, terms, var, scale):
-    end_low, end_high, jump_low, jump_high = terms
-    result = []
-    for i in range(6):
-        value = values[i] + float(scale * DM[i, 5]) * jump_high[var] - float(scale * DM[i, 0]) * jump_low[var]
-        if i == 0:
-            value = value + scale * end_low[var]
-        if i == 5:
-            value = value + scale * end_high[var]
-        result.append(value)
+        ends_low.append(low_flux[n] - visc * (low[3][n] - low[1][n]))
+        ends_high.append(visc * (high[3][n] - high[1][n]) - high_flux[n])
+        jumps.append(jump_parts(visc * (low[2][n] - low[0][n]), visc * (high[2][n] - high[0][n])))
+    return ends_low, ends_high, jumps
+
+
+def add_faces(values, terms, var):
+    ends_low, ends_high, jumps = terms
+    even, odd = jumps[var]
+    result = [None] * 6
+    for i in range(3):
+        result[i] = values[i] + (even[i] + odd[i])
+        result[5 - i] = values[5 - i] + (even[i] - odd[i])
+    result[0] = result[0] + ends_low[var]
+    result[5] = result[5] + ends_high[var]
     return result
 
 
@@ -208,7 +228,7 @@
             face0[1, (NV + v) * 6 + j] = last
         return carry
 
-    lax.fori_loop(0, 6, flow_row, 0)
+    rows_loop(6, 6, flow_row)
 
 
 def faces_span(field, face2):
@@ -222,7 +242,7 @@
             face2[1, (NV + v) * 5 + chunk] = last
         return carry
 
-    lax.fori_loop(0, 5, span_row, 0)
+    rows_loop(5, 5, span_row)
 
 
 def pack_faces(codes, face0, face2, flow_a, flow_b, span_a, span_b):
@@ -308,7 +328,7 @@
                 put_tile(prims, q * VROWS + row, values[q])
         return carry
 
-    lax.fori_loop(0, 9, primitives, 0)
+    rows_loop(9, 9, primitives)
 
 
 def volume_flow(section, field, register, codes, base, prims, face1, near1):
@@ -343,7 +363,7 @@
             face1[1, (NV + v) * 6 + i] = last
         return carry
 
-    lax.fori_loop(0, 6, wall_row, 0)
+    rows_loop(6, 6, wall_row)
 
 
 def volume_wall(field, codes, base, prims, face1, near1, face0, near0):
@@ -357,9 +377,10 @@
         terms = face_terms(low, high, 1)
         for v in range(NV):
             line = [tile_at(field, v * VROWS + row + j * 8) for j in range(6)]
-            second = second_derivative(line, step * VISCOSITY)
+            second = second_derivative(line, step * VISCOSITY, terms[2][v])
             values = [second[j] - float(step / WEIGHTS[j]) * sums[j][v] for j in range(6)]
-            values = add_faces(values, terms, v, step)
+            values[0] = values[0] + terms[0][v]
+            values[5] = values[5] + terms[1][v]
             for j in range(6):
                 where = v * VROWS + row + j * 8
                 put_tile(base, where, tile_at(base, where) + values[j])
@@ -389,7 +410,7 @@
 
 def surface_update(
     section, last, codes, field, base, face0, face2, near0, near2, received,
-    new_field, new_register, got0, got2, work,
+    new_field, new_register, got0, got2, work, *staging,
 ):
     flow_a, flow_b, span_a, span_b = received
     flow_odd, span_odd = lax.axis_index("px") & 1, lax.axis_index("py") & 1
@@ -398,7 +419,9 @@
     got0[1 - flow_odd] = flow_a[...]
     got0[flow_odd] = flow_b[pl.ds(0, 15)]
     surface_span(codes, base, face2, near2, got2, work)
-    surface_flow(section, last, codes, field, face0, near0, got0, new_field, new_register, work)
+    surface_flow(
+        section, last, codes, field, face0, near0, got0, new_field, new_register, work, *staging
+    )
 
 
 def sides(codes, first_side, own, near, tiles, t, got=None, groups=1):
@@ -424,43 +447,49 @@
 
 
 def surface_span(codes, base, face2, near2, got2, work):
-    step = TIME_STEP
-
     def span_row(chunk, carry):
         low, high = sides(codes, 4, face2, near2, 5, chunk, got2, 2)
         terms = face_terms(low, high, 2)
         for v in range(NV):
             values = [line_at(base, v, chunk, k) for k in range(6)]
-            values = add_faces(values, terms, v, step)
+            values = add_faces(values, terms, v)
             for k in range(6):
                 put_line(work, v, chunk, k, values[k])
         return carry
 
-    for chunk in range(5):
-        span_row(chunk, 0)
-
-
-def surface_flow(section, last, codes, field, face0, near0, got0, new_field, new_register, work):
-    step = TIME_STEP
+    rows_loop(5, 5, span_row)
+
+
+def surface_flow(
+    section, last, codes, field, face0, near0, got0, new_field, new_register, work,
+    out_state=None, out_register=None, sems=None,
+):
+    copies = []
 
     def flow_row(j, carry):
         low, high = sides(codes, 0, face0, near0, 6, j, got0, 4)
         terms = face_terms(low, high, 0)
         for v in range(NV):
             rows = [v * VROWS + i * 48 + j * 8 for i in range(6)]
-            values = add_faces([tile_at(work, row) for row in rows], terms, v, step)
+            values = add_faces([tile_at(work, row) for row in rows], terms, v)
             for i in range(6):
                 updated = tile_at(field, rows[i]) + RK_B[section] * values[i]
                 if last:
-                    new_field[v, i, j] = updated[:6]
-                    new_register[v, i, j] = values[i][:6]
+                    out_state[v, i, j] = updated[:6]
+                    out_register[v, i, j] = values[i][:6]
                 else:
                     put_tile(new_field, rows[i], updated)
                     put_tile(new_register, rows[i], values[i])
-        return carry
-
-    for j in range(6):
-        flow_row(j, 0)
+        if last:
+            for n, (source, target) in enumerate(((out_state, new_field), (out_register, new_register))):
+                copy = pltpu.make_async_copy(source.at[:, :, j], target.at[:, :, j], sems.at[n, j])
+                copy.start()
+                copies.append(copy)
+        return carry
+
+    rows_loop(6, 6, flow_row)
+    for copy in copies:
+        copy.wait()
 
 
 def surface_kernel(
@@ -478,11 +507,11 @@
 
 def last_kernel(
     section, codes, field, base, face0, face2, near0, near2, ra, rb, rc, rd,
-    advanced, register, got0, got2, work,
+    advanced, register, got0, got2, work, *staging,
 ):
     surface_update(
         section, True, codes, field, base, face0, face2, near0, near2, (ra, rb, rc, rd),
-        advanced, register, got0, got2, work,
+        advanced, register, got0, got2, work, *staging,
     )
 
 
@@ -560,16 +589,20 @@
         outs = [jax.ShapeDtypeStruct((NV, 6, 6, 6, 128), jnp.float32)] * 2
     else:
         outs = [vmem_out(FIELD), vmem_out(FIELD)] + face_outs()
+    scratch = [
+        pltpu.VMEM((2,) + FLOW_PACK, jnp.float32),
+        pltpu.VMEM((2,) + SPAN_PACK, jnp.float32),
+        pltpu.VMEM(FIELD, jnp.float32),
+    ]
+    if last:
+        scratch += [pltpu.VMEM((NV, 6, 6, 6, 128), jnp.float32)] * 2
+        scratch += [pltpu.SemaphoreType.DMA((2, 6))]
     return pl.pallas_call(
         kernel,
         out_shape=outs,
         in_specs=[VMEM_SPEC] * len(args),
-        out_specs=[VMEM_SPEC] * len(outs),
-        scratch_shapes=[
-            pltpu.VMEM((2,) + FLOW_PACK, jnp.float32),
-            pltpu.VMEM((2,) + SPAN_PACK, jnp.float32),
-            pltpu.VMEM(FIELD, jnp.float32),
-        ],
+        out_specs=[pl.BlockSpec(memory_space=pltpu.HBM) if last else VMEM_SPEC] * len(outs),
+        scratch_shapes=scratch,
         compiler_params=PARAMS,
         name="surface",
     )(*map(in_vmem, args))

time: 54.9 us -> 53.7 us (0.978)
  Pallas kernels: 22.5 us -> 20.3 us
  starting transfers between devices: 31 us -> 31.9 us
    pallas_call x5, Pallas kernels: 7.91 us -> 6.67 us  [surface_call(): pl.pallas_call(kernel, out_shape=outs, in_specs=[VMEM_SPEC] * len(args),...]
    ppermute x20, starting transfers between devices: 31 us -> 31.9 us  [swap(): return lax.ppermute(value, axis, pairs)]
    pallas_call x5, Pallas kernels: 12.8 us -> 11.9 us  [volume_call(): pl.pallas_call(kernel, out_shape=outs, in_specs=[VMEM_SPEC] * len(args),...]
  transfers between devices with their start and end apart: 20 -> 20, of which waited for: 1 -> 0; matrix products, arithmetic and copies ran while one was open for 0% -> 0% of each run, Pallas kernels for 23% -> 22%
where the time goes in v2:
time: 53.7 us; the launch traced here: 53.2 us
  starting transfers between devices  31.9 us (59%)
  Pallas kernels  20.3 us (38%)
  between operations  1.02 us (2%)
    ppermute x20, starting transfers between devices, swap(): return lax.ppermute(value, axis, pairs)  31.9 us
    pallas_call x5, Pallas kernels, volume_call(): pl.pallas_call(kernel, out_shape=outs, in_specs=[VMEM_SPEC] * len(args),...  11.9 us
    pallas_call x5, Pallas kernels, surface_call(): pl.pallas_call(kernel, out_shape=outs, in_specs=[VMEM_SPEC] * len(args),...  6.67 us
    pallas_call x1, Pallas kernels, first_call(): pl.pallas_call(first_kernel, out_shape=outs, in_specs=[pl.BlockSpec(memor...  1.7 us
  transfers between devices with their start and end apart: 20, of which 0 were waited for; matrix products, arithmetic and copies ran while one was open for 0% of the time, Pallas kernels for 22%

profile of v2, /device:TPU:1, one launch (start us, length us, event | category | flops | bytes accessed | tf_op | source)
XLA Modules:
  0.0 53.2 jit_solution(9048399322702088203)
XLA Ops:
  0.6 1.7 %first_faces.1 = (f32[1600,128]{1,0:T(8,128)S(1)}, s32[10,8,128]{2,1,0:T(8,128)S(1)}, f32[2,60,8,128]{3,2,1,0:T(8,128)S(1)}, f32[2,50,8,128]{3,2,1,0:T(8,128)S(1...) custom-call(f32[5,6,6,6,128]{4,3,2,1,0:T(8,128)} %conserved.1, ...), custom_call_target="tpu_custom_call" | custom-call | tf_op jit(solution)/shard_map/first_faces/pallas_call | solution.py:539
  2.3 7.1 %collective-permute-start.3 = (f32[26,8,128]{2,1,0:T(8,128)S(1)}, f32[26,8,128]{2,1,0:T(8,128)S(1)}, u32[]{:S(2)}, u32[]{:S(2)}) collective-permute-start(f32[26,8,128]{2,1,0:T(8,128)S(1)} %get-tuple-element.67), channel_id=1, source_target_pairs={{0,15},{1,2},{2,1},{3,4},{4,3},{5,6},{6,5},{7,8},{8,7},{9,10},{10,... | collective-permute-start | bytes 319496 | tf_op jit(solution)/shard_map/ppermute | solution.py:617
  9.5 2.1 %collective-permute-start.1 = (f32[16,8,128]{2,1,0:T(8,128)S(1)}, f32[16,8,128]{2,1,0:T(8,128)S(1)}, u32[]{:S(2)}, u32[]{:S(2)}) collective-permute-start(f32[16,8,128]{2,1,0:T(8,128)S(1)} %get-tuple-element.65), channel_id=1, source_target_pairs={{0,112},{16,32},{32,16},{48,64},{64,48},{80,96},{96,80},{112,0},{1... | collective-permute-start | bytes 196616 | tf_op jit(solution)/shard_map/ppermute | solution.py:617
  11.5 0.8 %collective-permute-start = (f32[15,8,128]{2,1,0:T(8,128)S(1)}, f32[15,8,128]{2,1,0:T(8,128)S(1)}, u32[]{:S(2)}, u32[]{:S(2)}) collective-permute-start(f32[15,8,128]{2,1,0:T(8,128)S(1)} %get-tuple-element.64), channel_id=1, source_target_pairs={{0,16},{16,0},{32,48},{48,32},{64,80},{80,64},{96,112},{112,96},{1... | collective-permute-start | bytes 184328 | tf_op jit(solution)/shard_map/ppermute | solution.py:617
  12.3 2.3 %volume.5 = (f32[1600,128]{1,0:T(8,128)S(1)}, f32[2,60,8,128]{3,2,1,0:T(8,128)S(1)}, f32[2,50,8,128]{3,2,1,0:T(8,128)S(1)}) custom-call(f32[1600,128]{1,0:T(8,128)S(1)} %get-tuple-element.58.refs_0_.refs_1_, s32[10,8,128]{2,1,0:T(8,128)S(1)} %get-tuple-element.57.refs_1_.refs_0_.refs_2_, f32[2,60,8,128]{3,2,1,0:T(8,128)S(1)} %get-tuple-element.59.refs_2_.refs_3_, ...), custom_call_target="tpu_custom_call" | custom-call | flops 10000000 | bytes 4000000 | tf_op jit(solution)/shard_map/volume/pallas_call | solution.py:566
  14.7 1.3 %surface.5 = (f32[1600,128]{1,0:T(8,128)S(1)}, f32[1600,128]{1,0:T(8,128)S(1)}, f32[2,60,8,128]{3,2,1,0:T(8,128)S(1)}, f32[2,50,8,128]{3,2,1,0:T(8,128)S(1)}, f3...) custom-call(s32[10,8,128]{2,1,0:T(8,128)S(1)} %get-tuple-element.57., ...), custom_call_target="tpu_custom_call" | custom-call | tf_op jit(solution)/shard_map/surface/pallas_call | solution.py:600
  16.0 1.7 %collective-permute-start.7 = (f32[26,8,128]{2,1,0:T(8,128)S(1)}, f32[26,8,128]{2,1,0:T(8,128)S(1)}, u32[]{:S(2)}, u32[]{:S(2)}) collective-permute-start(f32[26,8,128]{2,1,0:T(8,128)S(1)} %get-tuple-element.78), channel_id=1, source_target_pairs={{0,15},{1,2},{2,1},{3,4},{4,3},{5,6},{6,5},{7,8},{8,7},{9,10},{10,... | collective-permute-start | bytes 319496 | tf_op jit(solution)/shard_map/ppermute | solution.py:617
  17.7 3.2 %collective-permute-start.5 = (f32[16,8,128]{2,1,0:T(8,128)S(1)}, f32[16,8,128]{2,1,0:T(8,128)S(1)}, u32[]{:S(2)}, u32[]{:S(2)}) collective-permute-start(f32[16,8,128]{2,1,0:T(8,128)S(1)} %get-tuple-element.76), channel_id=1, source_target_pairs={{0,112},{16,32},{32,16},{48,64},{64,48},{80,96},{96,80},{112,0},{1... | collective-permute-start | bytes 196616 | tf_op jit(solution)/shard_map/ppermute | solution.py:617
  20.9 2.4 %volume.6 = (f32[1600,128]{1,0:T(8,128)S(1)}, f32[2,60,8,128]{3,2,1,0:T(8,128)S(1)}, f32[2,50,8,128]{3,2,1,0:T(8,128)S(1)}) custom-call(f32[1600,128]{1,0:T(8,128)S(1)} %get-tuple-element.68.refs_0_.refs_1_, f32[1600,128]{1,0:T(8,128)S(1)} %get-tuple-element.69.refs_1_, s32[10,8,128]{2,1,0:T(8,128)S(1)} %get-tuple-element.57.refs_1_.refs_0_.refs_2_, ...), custom_call_target="tpu_custom_call" | custom-call | flops 10000000 | bytes 4000000 | tf_op jit(solution)/shard_map/volume/pallas_call | solution.py:566
  23.3 1.3 %surface.6 = (f32[1600,128]{1,0:T(8,128)S(1)}, f32[1600,128]{1,0:T(8,128)S(1)}, f32[2,60,8,128]{3,2,1,0:T(8,128)S(1)}, f32[2,50,8,128]{3,2,1,0:T(8,128)S(1)}, f3...) custom-call(s32[10,8,128]{2,1,0:T(8,128)S(1)} %get-tuple-element.57., ...), custom_call_target="tpu_custom_call" | custom-call | tf_op jit(solution)/shard_map/surface/pallas_call | solution.py:600
  24.6 2.6 %collective-permute-start.11 = (f32[26,8,128]{2,1,0:T(8,128)S(1)}, f32[26,8,128]{2,1,0:T(8,128)S(1)}, u32[]{:S(2)}, u32[]{:S(2)}) collective-permute-start(f32[26,8,128]{2,1,0:T(8,128)S(1)} %get-tuple-element.89), channel_id=1, source_target_pairs={{0,15},{1,2},{2,1},{3,4},{4,3},{5,6},{6,5},{7,8},{8,7},{9,10},{10,... | collective-permute-start | bytes 319496 | tf_op jit(solution)/shard_map/ppermute | solution.py:617
  27.2 3.1 %collective-permute-start.9 = (f32[16,8,128]{2,1,0:T(8,128)S(1)}, f32[16,8,128]{2,1,0:T(8,128)S(1)}, u32[]{:S(2)}, u32[]{:S(2)}) collective-permute-start(f32[16,8,128]{2,1,0:T(8,128)S(1)} %get-tuple-element.87), channel_id=1, source_target_pairs={{0,112},{16,32},{32,16},{48,64},{64,48},{80,96},{96,80},{112,0},{1... | collective-permute-start | bytes 196616 | tf_op jit(solution)/shard_map/ppermute | solution.py:617
  30.3 2.4 %volume.7 = (f32[1600,128]{1,0:T(8,128)S(1)}, f32[2,60,8,128]{3,2,1,0:T(8,128)S(1)}, f32[2,50,8,128]{3,2,1,0:T(8,128)S(1)}) custom-call(f32[1600,128]{1,0:T(8,128)S(1)} %get-tuple-element.79.refs_0_.refs_1_, f32[1600,128]{1,0:T(8,128)S(1)} %get-tuple-element.80.refs_1_, s32[10,8,128]{2,1,0:T(8,128)S(1)} %get-tuple-element.57.refs_1_.refs_0_.refs_2_, ...), custom_call_target="tpu_custom_call" | custom-call | flops 10000000 | bytes 4000000 | tf_op jit(solution)/shard_map/volume/pallas_call | solution.py:566
  32.7 1.3 %surface.7 = (f32[1600,128]{1,0:T(8,128)S(1)}, f32[1600,128]{1,0:T(8,128)S(1)}, f32[2,60,8,128]{3,2,1,0:T(8,128)S(1)}, f32[2,50,8,128]{3,2,1,0:T(8,128)S(1)}, f3...) custom-call(s32[10,8,128]{2,1,0:T(8,128)S(1)} %get-tuple-element.57., ...), custom_call_target="tpu_custom_call" | custom-call | tf_op jit(solution)/shard_map/surface/pallas_call | solution.py:600
  34.0 1.8 %collective-permute-start.15 = (f32[26,8,128]{2,1,0:T(8,128)S(1)}, f32[26,8,128]{2,1,0:T(8,128)S(1)}, u32[]{:S(2)}, u32[]{:S(2)}) collective-permute-start(f32[26,8,128]{2,1,0:T(8,128)S(1)} %get-tuple-element.100), channel_id=1, source_target_pairs={{0,15},{1,2},{2,1},{3,4},{4,3},{5,6},{6,5},{7,8},{8,7},{9,10},{10,... | collective-permute-start | bytes 319496 | tf_op jit(solution)/shard_map/ppermute | solution.py:617
  35.8 0.1 collective-permute-start.14
  35.9 3.7 %collective-permute-start.13 = (f32[16,8,128]{2,1,0:T(8,128)S(1)}, f32[16,8,128]{2,1,0:T(8,128)S(1)}, u32[]{:S(2)}, u32[]{:S(2)}) collective-permute-start(f32[16,8,128]{2,1,0:T(8,128)S(1)} %get-tuple-element.98), channel_id=1, source_target_pairs={{0,112},{16,32},{32,16},{48,64},{64,48},{80,96},{96,80},{112,0},{1... | collective-permute-start | bytes 196616 | tf_op jit(solution)/shard_map/ppermute | solution.py:617
  39.6 2.4 %volume.8 = (f32[1600,128]{1,0:T(8,128)S(1)}, f32[2,60,8,128]{3,2,1,0:T(8,128)S(1)}, f32[2,50,8,128]{3,2,1,0:T(8,128)S(1)}) custom-call(f32[1600,128]{1,0:T(8,128)S(1)} %get-tuple-element.90.refs_0_.refs_1_, f32[1600,128]{1,0:T(8,128)S(1)} %get-tuple-element.91.refs_1_, s32[10,8,128]{2,1,0:T(8,128)S(1)} %get-tuple-element.57.refs_1_.refs_0_.refs_2_, ...), custom_call_target="tpu_custom_call" | custom-call | flops 10000000 | bytes 4000000 | tf_op jit(solution)/shard_map/volume/pallas_call | solution.py:566
  42.1 1.3 %surface.8 = (f32[1600,128]{1,0:T(8,128)S(1)}, f32[1600,128]{1,0:T(8,128)S(1)}, f32[2,60,8,128]{3,2,1,0:T(8,128)S(1)}, f32[2,50,8,128]{3,2,1,0:T(8,128)S(1)}, f3...) custom-call(s32[10,8,128]{2,1,0:T(8,128)S(1)} %get-tuple-element.57., ...), custom_call_target="tpu_custom_call" | custom-call | tf_op jit(solution)/shard_map/surface/pallas_call | solution.py:600
  43.3 1.8 %collective-permute-start.19 = (f32[26,8,128]{2,1,0:T(8,128)S(1)}, f32[26,8,128]{2,1,0:T(8,128)S(1)}, u32[]{:S(2)}, u32[]{:S(2)}) collective-permute-start(f32[26,8,128]{2,1,0:T(8,128)S(1)} %get-tuple-element.111), channel_id=1, source_target_pairs={{0,15},{1,2},{2,1},{3,4},{4,3},{5,6},{6,5},{7,8},{8,7},{9,10},{10,... | collective-permute-start | bytes 319496 | tf_op jit(solution)/shard_map/ppermute | solution.py:617
  45.1 0.1 collective-permute-start.18
  45.3 3.7 %collective-permute-start.17 = (f32[16,8,128]{2,1,0:T(8,128)S(1)}, f32[16,8,128]{2,1,0:T(8,128)S(1)}, u32[]{:S(2)}, u32[]{:S(2)}) collective-permute-start(f32[16,8,128]{2,1,0:T(8,128)S(1)} %get-tuple-element.109), channel_id=1, source_target_pairs={{0,112},{16,32},{32,16},{48,64},{64,48},{80,96},{96,80},{112,0},{1... | collective-permute-start | bytes 196616 | tf_op jit(solution)/shard_map/ppermute | solution.py:617
  49.0 2.4 %volume.9 = (f32[1600,128]{1,0:T(8,128)S(1)}, f32[2,60,8,128]{3,2,1,0:T(8,128)S(1)}, f32[2,50,8,128]{3,2,1,0:T(8,128)S(1)}) custom-call(f32[1600,128]{1,0:T(8,128)S(1)} %get-tuple-element.101.refs_0_.refs_1_, f32[1600,128]{1,0:T(8,128)S(1)} %get-tuple-element.102.refs_1_, s32[10,8,128]{2,1,0:T(8,128)S(1)} %get-tuple-element.57.refs_1_.refs_0_.refs_2_, ...), custom_call_target="tpu_custom_call" | custom-call | flops 10000000 | bytes 4000000 | tf_op jit(solution)/shard_map/volume/pallas_call | solution.py:566
  51.4 1.6 %surface.9 = (f32[5,6,6,6,128]{4,3,2,1,0:T(8,128)}, f32[5,6,6,6,128]{4,3,2,1,0:T(8,128)}) custom-call(s32[10,8,128]{2,1,0:T(8,128)S(1)} %get-tuple-element.57.refs_1_.refs_0_.refs_2_, f32[1600,128]{1,0:T(8,128)S(1)} %get-tuple-element.101.refs_0_.refs_1_, f32[1600,128]{1,0:T(8,128)S(1)} %get-tuple-element.105.refs_2_, ...), custom_call_target="tpu_custom_call" | custom-call | tf_op jit(solution)/shard_map/surface/pallas_call | solution.py:600
  (27 shorter events, 0.1 us)
Async XLA Ops:
  2.3 12.4 %collective-permute-start.3 = (f32[26,8,128]{2,1,0:T(8,128)S(1)}, f32[26,8,128]{2,1,0:T(8,128)S(1)}, u32[]{:S(2)}, u32[]{:S(2)}) collective-permute-start(f32[26,8,128]{2,1,0:T(8,128)S(1)} %get-tuple-element.67), channel_id=1, source_target_pairs={{0,15},{1,2},{2,1},{3,4},{4,3},{5,6},{6,5},{7,8},{8,7},{9,10},{10,... | collective-permute-start | bytes 319496 | tf_op jit(solution)/shard_map/ppermute | solution.py:617
  9.5 5.2 %collective-permute-start.2 = (f32[25,8,128]{2,1,0:T(8,128)S(1)}, f32[25,8,128]{2,1,0:T(8,128)S(1)}, u32[]{:S(2)}, u32[]{:S(2)}) collective-permute-start(f32[25,8,128]{2,1,0:T(8,128)S(1)} %get-tuple-element.66), channel_id=1, source_target_pairs={{0,1},{1,0},{2,3},{3,2},{4,5},{5,4},{6,7},{7,6},{8,9},{9,8},{10,11... | collective-permute-start | bytes 307208 | tf_op jit(solution)/shard_map/ppermute | solution.py:617
  9.5 5.2 %collective-permute-start.1 = (f32[16,8,128]{2,1,0:T(8,128)S(1)}, f32[16,8,128]{2,1,0:T(8,128)S(1)}, u32[]{:S(2)}, u32[]{:S(2)}) collective-permute-start(f32[16,8,128]{2,1,0:T(8,128)S(1)} %get-tuple-element.65), channel_id=1, source_target_pairs={{0,112},{16,32},{32,16},{48,64},{64,48},{80,96},{96,80},{112,0},{1... | collective-permute-start | bytes 196616 | tf_op jit(solution)/shard_map/ppermute | solution.py:617
  11.5 3.2 %collective-permute-start = (f32[15,8,128]{2,1,0:T(8,128)S(1)}, f32[15,8,128]{2,1,0:T(8,128)S(1)}, u32[]{:S(2)}, u32[]{:S(2)}) collective-permute-start(f32[15,8,128]{2,1,0:T(8,128)S(1)} %get-tuple-element.64), channel_id=1, source_target_pairs={{0,16},{16,0},{32,48},{48,32},{64,80},{80,64},{96,112},{112,96},{1... | collective-permute-start | bytes 184328 | tf_op jit(solution)/shard_map/ppermute | solution.py:617
  16.0 7.3 %collective-permute-start.7 = (f32[26,8,128]{2,1,0:T(8,128)S(1)}, f32[26,8,128]{2,1,0:T(8,128)S(1)}, u32[]{:S(2)}, u32[]{:S(2)}) collective-permute-start(f32[26,8,128]{2,1,0:T(8,128)S(1)} %get-tuple-element.78), channel_id=1, source_target_pairs={{0,15},{1,2},{2,1},{3,4},{4,3},{5,6},{6,5},{7,8},{8,7},{9,10},{10,... | collective-permute-start | bytes 319496 | tf_op jit(solution)/shard_map/ppermute | solution.py:617
  17.7 5.6 %collective-permute-start.6 = (f32[25,8,128]{2,1,0:T(8,128)S(1)}, f32[25,8,128]{2,1,0:T(8,128)S(1)}, u32[]{:S(2)}, u32[]{:S(2)}) collective-permute-start(f32[25,8,128]{2,1,0:T(8,128)S(1)} %get-tuple-element.77), channel_id=1, source_target_pairs={{0,1},{1,0},{2,3},{3,2},{4,5},{5,4},{6,7},{7,6},{8,9},{9,8},{10,11... | collective-permute-start | bytes 307208 | tf_op jit(solution)/shard_map/ppermute | solution.py:617
  17.7 5.6 %collective-permute-start.5 = (f32[16,8,128]{2,1,0:T(8,128)S(1)}, f32[16,8,128]{2,1,0:T(8,128)S(1)}, u32[]{:S(2)}, u32[]{:S(2)}) collective-permute-start(f32[16,8,128]{2,1,0:T(8,128)S(1)} %get-tuple-element.76), channel_id=1, source_target_pairs={{0,112},{16,32},{32,16},{48,64},{64,48},{80,96},{96,80},{112,0},{1... | collective-permute-start | bytes 196616 | tf_op jit(solution)/shard_map/ppermute | solution.py:617
  20.9 2.4 %collective-permute-start.4 = (f32[15,8,128]{2,1,0:T(8,128)S(1)}, f32[15,8,128]{2,1,0:T(8,128)S(1)}, u32[]{:S(2)}, u32[]{:S(2)}) collective-permute-start(f32[15,8,128]{2,1,0:T(8,128)S(1)} %get-tuple-element.75), channel_id=1, source_target_pairs={{0,16},{16,0},{32,48},{48,32},{64,80},{80,64},{96,112},{112,96},{1... | collective-permute-start | bytes 184328 | tf_op jit(solution)/shard_map/ppermute | solution.py:617
  24.6 8.1 %collective-permute-start.11 = (f32[26,8,128]{2,1,0:T(8,128)S(1)}, f32[26,8,128]{2,1,0:T(8,128)S(1)}, u32[]{:S(2)}, u32[]{:S(2)}) collective-permute-start(f32[26,8,128]{2,1,0:T(8,128)S(1)} %get-tuple-element.89), channel_id=1, source_target_pairs={{0,15},{1,2},{2,1},{3,4},{4,3},{5,6},{6,5},{7,8},{8,7},{9,10},{10,... | collective-permute-start | bytes 319496 | tf_op jit(solution)/shard_map/ppermute | solution.py:617
  27.2 5.5 %collective-permute-start.10 = (f32[25,8,128]{2,1,0:T(8,128)S(1)}, f32[25,8,128]{2,1,0:T(8,128)S(1)}, u32[]{:S(2)}, u32[]{:S(2)}) collective-permute-start(f32[25,8,128]{2,1,0:T(8,128)S(1)} %get-tuple-element.88), channel_id=1, source_target_pairs={{0,1},{1,0},{2,3},{3,2},{4,5},{5,4},{6,7},{7,6},{8,9},{9,8},{10,11... | collective-permute-start | bytes 307208 | tf_op jit(solution)/shard_map/ppermute | solution.py:617
  27.2 5.5 %collective-permute-start.9 = (f32[16,8,128]{2,1,0:T(8,128)S(1)}, f32[16,8,128]{2,1,0:T(8,128)S(1)}, u32[]{:S(2)}, u32[]{:S(2)}) collective-permute-start(f32[16,8,128]{2,1,0:T(8,128)S(1)} %get-tuple-element.87), channel_id=1, source_target_pairs={{0,112},{16,32},{32,16},{48,64},{64,48},{80,96},{96,80},{112,0},{1... | collective-permute-start | bytes 196616 | tf_op jit(solution)/shard_map/ppermute | solution.py:617
  30.3 2.4 %collective-permute-start.8 = (f32[15,8,128]{2,1,0:T(8,128)S(1)}, f32[15,8,128]{2,1,0:T(8,128)S(1)}, u32[]{:S(2)}, u32[]{:S(2)}) collective-permute-start(f32[15,8,128]{2,1,0:T(8,128)S(1)} %get-tuple-element.86), channel_id=1, source_target_pairs={{0,16},{16,0},{32,48},{48,32},{64,80},{80,64},{96,112},{112,96},{1... | collective-permute-start | bytes 184328 | tf_op jit(solution)/shard_map/ppermute | solution.py:617
  34.0 8.1 %collective-permute-start.15 = (f32[26,8,128]{2,1,0:T(8,128)S(1)}, f32[26,8,128]{2,1,0:T(8,128)S(1)}, u32[]{:S(2)}, u32[]{:S(2)}) collective-permute-start(f32[26,8,128]{2,1,0:T(8,128)S(1)} %get-tuple-element.100), channel_id=1, source_target_pairs={{0,15},{1,2},{2,1},{3,4},{4,3},{5,6},{6,5},{7,8},{8,7},{9,10},{10,... | collective-permute-start | bytes 319496 | tf_op jit(solution)/shard_map/ppermute | solution.py:617
  35.8 6.3 %collective-permute-start.14 = (f32[25,8,128]{2,1,0:T(8,128)S(1)}, f32[25,8,128]{2,1,0:T(8,128)S(1)}, u32[]{:S(2)}, u32[]{:S(2)}) collective-permute-start(f32[25,8,128]{2,1,0:T(8,128)S(1)} %get-tuple-element.99), channel_id=1, source_target_pairs={{0,1},{1,0},{2,3},{3,2},{4,5},{5,4},{6,7},{7,6},{8,9},{9,8},{10,11... | collective-permute-start | bytes 307208 | tf_op jit(solution)/shard_map/ppermute | solution.py:617
  35.9 6.2 %collective-permute-start.13 = (f32[16,8,128]{2,1,0:T(8,128)S(1)}, f32[16,8,128]{2,1,0:T(8,128)S(1)}, u32[]{:S(2)}, u32[]{:S(2)}) collective-permute-start(f32[16,8,128]{2,1,0:T(8,128)S(1)} %get-tuple-element.98), channel_id=1, source_target_pairs={{0,112},{16,32},{32,16},{48,64},{64,48},{80,96},{96,80},{112,0},{1... | collective-permute-start | bytes 196616 | tf_op jit(solution)/shard_map/ppermute | solution.py:617
  39.6 2.4 %collective-permute-start.12 = (f32[15,8,128]{2,1,0:T(8,128)S(1)}, f32[15,8,128]{2,1,0:T(8,128)S(1)}, u32[]{:S(2)}, u32[]{:S(2)}) collective-permute-start(f32[15,8,128]{2,1,0:T(8,128)S(1)} %get-tuple-element.97), channel_id=1, source_target_pairs={{0,16},{16,0},{32,48},{48,32},{64,80},{80,64},{96,112},{112,96},{1... | collective-permute-start | bytes 184328 | tf_op jit(solution)/shard_map/ppermute | solution.py:617
  43.3 8.1 %collective-permute-start.19 = (f32[26,8,128]{2,1,0:T(8,128)S(1)}, f32[26,8,128]{2,1,0:T(8,128)S(1)}, u32[]{:S(2)}, u32[]{:S(2)}) collective-permute-start(f32[26,8,128]{2,1,0:T(8,128)S(1)} %get-tuple-element.111), channel_id=1, source_target_pairs={{0,15},{1,2},{2,1},{3,4},{4,3},{5,6},{6,5},{7,8},{8,7},{9,10},{10,... | collective-permute-start | bytes 319496 | tf_op jit(solution)/shard_map/ppermute | solution.py:617
  45.1 6.3 %collective-permute-start.18 = (f32[25,8,128]{2,1,0:T(8,128)S(1)}, f32[25,8,128]{2,1,0:T(8,128)S(1)}, u32[]{:S(2)}, u32[]{:S(2)}) collective-permute-start(f32[25,8,128]{2,1,0:T(8,128)S(1)} %get-tuple-element.110), channel_id=1, source_target_pairs={{0,1},{1,0},{2,3},{3,2},{4,5},{5,4},{6,7},{7,6},{8,9},{9,8},{10,11... | collective-permute-start | bytes 307208 | tf_op jit(solution)/shard_map/ppermute | solution.py:617
  45.3 6.2 %collective-permute-start.17 = (f32[16,8,128]{2,1,0:T(8,128)S(1)}, f32[16,8,128]{2,1,0:T(8,128)S(1)}, u32[]{:S(2)}, u32[]{:S(2)}) collective-permute-start(f32[16,8,128]{2,1,0:T(8,128)S(1)} %get-tuple-element.109), channel_id=1, source_target_pairs={{0,112},{16,32},{32,16},{48,64},{64,48},{80,96},{96,80},{112,0},{1... | collective-permute-start | bytes 196616 | tf_op jit(solution)/shard_map/ppermute | solution.py:617
  49.0 2.4 %collective-permute-start.16 = (f32[15,8,128]{2,1,0:T(8,128)S(1)}, f32[15,8,128]{2,1,0:T(8,128)S(1)}, u32[]{:S(2)}, u32[]{:S(2)}) collective-permute-start(f32[15,8,128]{2,1,0:T(8,128)S(1)} %get-tuple-element.108), channel_id=1, source_target_pairs={{0,16},{16,0},{32,48},{48,32},{64,80},{80,64},{96,112},{112,96},{1... | collective-permute-start | bytes 184328 | tf_op jit(solution)/shard_map/ppermute | solution.py:617

commit v3 on v2

--- a/solution.py
+++ b/solution.py
@@ -49,11 +49,11 @@
 VROWS = 320
 FIELD = (NV * VROWS, 128)
 FACE0 = (2, 60, 8, 128)
-FACE2 = (2, 50, 8, 128)
+FACE2 = (2, 55, 8, 128)
 FLOW_PACK = (15, 8, 128)
-SPAN_PACK = (25, 8, 128)
+SPAN_PACK = (23, 8, 128)
 FLOW_FAR = (16, 8, 128)
-SPAN_FAR = (26, 8, 128)
+SPAN_FAR = (24, 8, 128)
 CODES = (10, 8, 128)
 RECEIVED = 256
 WALL = 512
@@ -85,6 +85,10 @@
         step(0, 0)
     else:
         lax.fori_loop(0, count // unroll, step, 0)
+
+
+def span_place(q, chunk):
+    return q * 4 + chunk if chunk < 4 else 40 + q // 2
 
 
 def take_lanes(value, index):
@@ -212,11 +216,6 @@
     return result
 
 
-def make_faces(field, face0, face2):
-    faces_flow(field, face0)
-    faces_span(field, face2)
-
-
 def faces_flow(field, face0):
     def flow_row(j, carry):
         for v in range(NV):
@@ -232,40 +231,58 @@
 
 
 def faces_span(field, face2):
-    def span_row(chunk, carry):
+    upper = lax.broadcasted_iota(jnp.int32, (8, 128), 0) >= 4
+    for chunk in range(5):
+        ends = [[None] * (2 * NV), [None] * (2 * NV)]
         for v in range(NV):
             values = [line_at(field, v, chunk, k) for k in range(6)]
-            first, last = end_derivatives(values)
-            face2[0, v * 5 + chunk] = values[0]
-            face2[1, v * 5 + chunk] = values[5]
-            face2[0, (NV + v) * 5 + chunk] = first
-            face2[1, (NV + v) * 5 + chunk] = last
-        return carry
-
-    rows_loop(5, 5, span_row)
-
-
-def pack_faces(codes, face0, face2, flow_a, flow_b, span_a, span_b):
+            ends[0][v], ends[1][v] = values[0], values[5]
+            ends[0][NV + v], ends[1][NV + v] = end_derivatives(values)
+        for side in range(2):
+            for q in range(2 * NV):
+                face2[side, q * 5 + chunk] = ends[side][q]
+                if chunk == 4 and q % 2:
+                    shifted = pltpu.roll(ends[side][q], 4, 0)
+                    face2[side, 50 + q // 2] = jnp.where(upper, shifted, ends[side][q - 1])
+
+
+def pack_span(codes, side, face2, out):
     lane = lax.broadcasted_iota(jnp.int32, (8, 128), 1)
+    index = codes[8 + side]
+    rows = [q * 5 + chunk for q in range(2 * NV) for chunk in range(4)] + list(range(50, 55))
+    for t in range(23):
+        packed = take_lanes(face2[side, rows[t]], index)
+        if 23 + t < 45:
+            packed = jnp.where(lane >= 64, take_lanes(face2[side, rows[23 + t]], index), packed)
+        out[t] = packed
+
+
+def pack_flow(codes, side, face0, out):
+    lane = lax.broadcasted_iota(jnp.int32, (8, 128), 1)
+    index = codes[6 + side]
+    for t in range(15):
+        packed = take_lanes(face0[side, t], index)
+        for g in range(1, 4):
+            packed = jnp.where(lane >= 32 * g, take_lanes(face0[side, 15 * g + t], index), packed)
+        out[t] = packed
+
+
+def far_faces(field, codes, face2, span_b):
+    faces_span(field, face2)
+    pack_span(codes, lax.axis_index("py") & 1, face2, span_b)
+
+
+def near_kernel(field, codes, face2, face0, flow_a, flow_b, span_a):
     flow_odd, span_odd = lax.axis_index("px") & 1, lax.axis_index("py") & 1
-    for side, out in ((1 - span_odd, span_a), (span_odd, span_b)):
-        index = codes[8 + side]
-        for t in range(25):
-            out[t] = jnp.where(
-                lane >= 64, take_lanes(face2[side, 25 + t], index), take_lanes(face2[side, t], index)
-            )
-    for side, out in ((1 - flow_odd, flow_a), (flow_odd, flow_b)):
-        index = codes[6 + side]
-        for t in range(15):
-            packed = take_lanes(face0[side, t], index)
-            for g in range(1, 4):
-                packed = jnp.where(lane >= 32 * g, take_lanes(face0[side, 15 * g + t], index), packed)
-            out[t] = packed
+    faces_flow(field, face0)
+    pack_span(codes, 1 - span_odd, face2, span_a)
+    pack_flow(codes, flow_odd, face0, flow_b)
+    pack_flow(codes, 1 - flow_odd, face0, flow_a)
 
 
 def first_kernel(
-    conserved, flow_lists, span_lists, face_source, field, codes, face0, face2,
-    flow_a, flow_b, span_a, span_b, state, flow_rows, span_rows, columns, list_sems, state_sems,
+    conserved, flow_lists, span_lists, face_source, field, codes, face2, span_b,
+    state, flow_rows, span_rows, columns, list_sems, state_sems,
 ):
     copies = [
         pltpu.make_async_copy(source, target, list_sems.at[n])
@@ -298,8 +315,7 @@
         for i in range(6):
             for j in range(6):
                 field[pl.ds(v * VROWS + i * 48 + j * 8, 6), :] = state[v, i, j]
-    make_faces(field, face0, face2)
-    pack_faces(codes, face0, face2, flow_a, flow_b, span_a, span_b)
+    far_faces(field, codes, face2, span_b)
 
 
 def volume_kernel(
@@ -415,7 +431,7 @@
     flow_a, flow_b, span_a, span_b = received
     flow_odd, span_odd = lax.axis_index("px") & 1, lax.axis_index("py") & 1
     got2[1 - span_odd] = span_a[...]
-    got2[span_odd] = span_b[pl.ds(0, 25)]
+    got2[span_odd] = span_b[pl.ds(0, 23)]
     got0[1 - flow_odd] = flow_a[...]
     got0[flow_odd] = flow_b[pl.ds(0, 15)]
     surface_span(codes, base, face2, near2, got2, work)
@@ -436,9 +452,12 @@
             own_value = own[side, row]
             other_value = near[side, row]
             if got is not None:
-                share = 2 * NV * tiles // groups
-                index = (code + (128 // groups) * (row // share)) & 127
-                other_value = jnp.where(received, take_lanes(got[side, row % share], index), other_value)
+                place, share = (span_place(q, t), 23) if groups == 2 else (row, 15)
+                index = (code + (128 // groups) * (place // share)) & 127
+                taken = take_lanes(got[side, place % share], index)
+                if groups == 2 and t == 4 and q % 2:
+                    taken = pltpu.roll(taken, 4, 0)
+                other_value = jnp.where(received, taken, other_value)
             mirrored = -own_value if 1 <= q <= 3 else own_value
             own_values.append(own_value)
             other_values.append(jnp.where(wall, mirrored, other_value))
@@ -494,15 +513,13 @@
 
 def surface_kernel(
     section, codes, field, base, face0, face2, near0, near2, ra, rb, rc, rd,
-    new_field, new_register, new_face0, new_face2, flow_a, flow_b, span_a, span_b,
-    got0, got2, work,
+    new_field, new_register, new_face2, span_b, got0, got2, work,
 ):
     surface_update(
         section, False, codes, field, base, face0, face2, near0, near2, (ra, rb, rc, rd),
         new_field, new_register, got0, got2, work,
     )
-    make_faces(new_field, new_face0, new_face2)
-    pack_faces(codes, new_face0, new_face2, flow_a, flow_b, span_a, span_b)
+    far_faces(new_field, codes, new_face2, span_b)
 
 
 def last_kernel(
@@ -527,15 +544,21 @@
     return pltpu.VMEM(shape, dtype)
 
 
-def face_outs():
-    return [
-        vmem_out(FACE0), vmem_out(FACE2), vmem_out(FLOW_PACK), vmem_out(FLOW_FAR),
-        vmem_out(SPAN_PACK), vmem_out(SPAN_FAR),
-    ]
+def near_call(field, codes, face2):
+    shapes = (FACE0, FLOW_PACK, FLOW_FAR, SPAN_PACK)
+    return pl.pallas_call(
+        near_kernel,
+        out_shape=[vmem_out(shape) for shape in shapes],
+        in_specs=[VMEM_SPEC] * 3,
+        out_specs=[VMEM_SPEC] * len(shapes),
+        compiler_params=PARAMS,
+        cost_estimate=pl.CostEstimate(flops=10**6, bytes_accessed=10**6, transcendentals=0),
+        name="near_faces",
+    )(*map(in_vmem, (field, codes, face2)))
 
 
 def first_call(*args):
-    outs = [vmem_out(FIELD), vmem_out(CODES, jnp.int32)] + face_outs()
+    outs = [vmem_out(FIELD), vmem_out(CODES, jnp.int32), vmem_out(FACE2), vmem_out(SPAN_FAR)]
     return pl.pallas_call(
         first_kernel,
         out_shape=outs,
@@ -574,7 +597,7 @@
             pltpu.VMEM(FACE0, jnp.float32),
         ],
         compiler_params=PARAMS,
-        cost_estimate=pl.CostEstimate(flops=10**7, bytes_accessed=4 * 10**6, transcendentals=0),
+        cost_estimate=pl.CostEstimate(flops=10**4, bytes_accessed=10**4, transcendentals=0),
         name="volume",
     )(*map(in_vmem, args))
 
@@ -588,7 +611,7 @@
     if last:
         outs = [jax.ShapeDtypeStruct((NV, 6, 6, 6, 128), jnp.float32)] * 2
     else:
-        outs = [vmem_out(FIELD), vmem_out(FIELD)] + face_outs()
+        outs = [vmem_out(FIELD), vmem_out(FIELD), vmem_out(FACE2), vmem_out(SPAN_FAR)]
     scratch = [
         pltpu.VMEM((2,) + FLOW_PACK, jnp.float32),
         pltpu.VMEM((2,) + SPAN_PACK, jnp.float32),
@@ -618,11 +641,11 @@
 
 
 def body(conserved, flow_lists, span_lists, face_source):
-    field, codes, *faces = first_call(conserved, flow_lists, span_lists, face_source)
+    field, codes, face2, span_b = first_call(conserved, flow_lists, span_lists, face_source)
     register = None
     for section in range(len(RK_A)):
-        face0, face2, flow_a, flow_b, span_a, span_b = faces
         rd = swap(span_b, "py", True)
+        face0, flow_a, flow_b, span_a = near_call(field, codes, face2)
         rc = swap(span_a, "py", False)
         rb = swap(flow_b, "px", True)
         ra = swap(flow_a, "px", False)
@@ -632,7 +655,7 @@
         )
         if section == len(RK_A) - 1:
             return tuple(outs)
-        field, register, *faces = outs
+        field, register, face2, span_b = outs
 
 
 def solution(mesh):

time: 53.7 us -> 53.5 us (level)
    pallas_call x0 -> x5, Pallas kernels: none -> 1.4 us  [near_call(): pl.pallas_call(near_kernel, out_shape=[vmem_out(shape) for shape in shape...]
    pallas_call x5, Pallas kernels: 6.67 us -> 5.98 us  [surface_call(): pl.pallas_call(kernel, out_shape=outs, in_specs=[VMEM_SPEC] * len(args),...]
  transfers between devices with their start and end apart: 20 -> 20, of which waited for: 0 -> 0; matrix products, arithmetic and copies ran while one was open for 0% -> 0% of each run, Pallas kernels for 22% -> 25%
where the time goes in v3:
time: 53.5 us; the launch traced here: 53.3 us
  starting transfers between devices  31.4 us (59%)
  Pallas kernels  20.8 us (39%)
  between operations  1.06 us (2%)
    ppermute x20, starting transfers between devices, swap(): return lax.ppermute(value, axis, pairs)  31.4 us
    pallas_call x5, Pallas kernels, volume_call(): pl.pallas_call(kernel, out_shape=outs, in_specs=[VMEM_SPEC] * len(args),...  11.9 us
    pallas_call x5, Pallas kernels, surface_call(): pl.pallas_call(kernel, out_shape=outs, in_specs=[VMEM_SPEC] * len(args),...  5.98 us
    pallas_call x1, Pallas kernels, first_call(): pl.pallas_call(first_kernel, out_shape=outs, in_specs=[pl.BlockSpec(memor...  1.49 us
    pallas_call x5, Pallas kernels, near_call(): pl.pallas_call(near_kernel, out_shape=[vmem_out(shape) for shape in shape...  1.4 us
  transfers between devices with their start and end apart: 20, of which 0 were waited for; matrix products, arithmetic and copies ran while one was open for 0% of the time, Pallas kernels for 25%

profile of v3, /device:TPU:1, one launch (start us, length us, event | category | flops | bytes accessed | tf_op | source)
XLA Modules:
  0.0 53.3 jit_solution(12690670830438498792)
XLA Ops:
  0.6 1.5 %first_faces.1 = (f32[1600,128]{1,0:T(8,128)S(1)}, s32[10,8,128]{2,1,0:T(8,128)S(1)}, f32[2,55,8,128]{3,2,1,0:T(8,128)S(1)}, f32[24,8,128]{2,1,0:T(8,128)S(1)}) custom-call(f32[5,6,6,6,128]{4,3,2,1,0:T(8,128)} %conserved.1, s32[1,2,32]{2,1,0:T(2,128)} %flow_lists.1, s32[1,2,64]{2,1,0:T(2,128)} %span_lists.1, s32[6,128]{1,0:T(8,128)} %face_source.1), custom_call_target="tpu_custom_call" | custom-call | tf_op jit(solution)/shard_map/first_faces/pallas_call | solution.py:562
  2.1 7.1 %collective-permute-start.3 = (f32[24,8,128]{2,1,0:T(8,128)S(1)}, f32[24,8,128]{2,1,0:T(8,128)S(1)}, u32[]{:S(2)}, u32[]{:S(2)}) collective-permute-start(f32[24,8,128]{2,1,0:T(8,128)S(1)} %get-tuple-element.67), channel_id=1, source_target_pairs={{0,15},{1,2},{2,1},{3,4},{4,3},{5,6},{6,5},{7,8},{8,7},{9,10},{10,... | collective-permute-start | bytes 294920 | tf_op jit(solution)/shard_map/ppermute | solution.py:640
  9.6 2.1 %collective-permute-start.1 = (f32[16,8,128]{2,1,0:T(8,128)S(1)}, f32[16,8,128]{2,1,0:T(8,128)S(1)}, u32[]{:S(2)}, u32[]{:S(2)}) collective-permute-start(f32[16,8,128]{2,1,0:T(8,128)S(1)} %get-tuple-element.65), channel_id=1, source_target_pairs={{0,112},{16,32},{32,16},{48,64},{64,48},{80,96},{96,80},{112,0},{1... | collective-permute-start | bytes 196616 | tf_op jit(solution)/shard_map/ppermute | solution.py:640
  11.8 0.8 %collective-permute-start = (f32[15,8,128]{2,1,0:T(8,128)S(1)}, f32[15,8,128]{2,1,0:T(8,128)S(1)}, u32[]{:S(2)}, u32[]{:S(2)}) collective-permute-start(f32[15,8,128]{2,1,0:T(8,128)S(1)} %get-tuple-element.64), channel_id=1, source_target_pairs={{0,16},{16,0},{32,48},{48,32},{64,80},{80,64},{96,112},{112,96},{1... | collective-permute-start | bytes 184328 | tf_op jit(solution)/shard_map/ppermute | solution.py:640
  12.6 2.3 %volume.5 = (f32[1600,128]{1,0:T(8,128)S(1)}, f32[2,60,8,128]{3,2,1,0:T(8,128)S(1)}, f32[2,55,8,128]{3,2,1,0:T(8,128)S(1)}) custom-call(f32[1600,128]{1,0:T(8,128)S(1)} %get-tuple-element.58.field.refs_0_.refs_1_, s32[10,8,128]{2,1,0:T(8,128)S(1)} %get-tuple-element.57.codes.refs_1_.refs_0_.refs_2_, f32[2,60,8,128]{3,2,1,0:T(8,128)S(1)} %get-tuple-element.60.refs_2_.refs_3_, ...), custom_call_target="tpu_custom_call" | custom-call | flops 10000 | bytes 10000 | tf_op jit(solution)/shard_map/volume/pallas_call | solution.py:589
  15.0 1.1 %surface.5 = (f32[1600,128]{1,0:T(8,128)S(1)}, f32[1600,128]{1,0:T(8,128)S(1)}, f32[2,55,8,128]{3,2,1,0:T(8,128)S(1)}, f32[24,8,128]{2,1,0:T(8,128)S(1)}) custom-call(s32[10,8,128]{2,1,0:T(8,128)S(1)} %get-tuple-element.57.codes.refs_1_.refs_0_.refs_2_, f32[1600,128]{1,0:T(8,128)S(1)} %get-tuple-element.58.field.refs_0_.refs_1_, ...), custom_call_target="tpu_custom_call" | custom-call | tf_op jit(solution)/shard_map/surface/pallas_call | solution.py:623
  16.1 1.1 %collective-permute-start.7 = (f32[24,8,128]{2,1,0:T(8,128)S(1)}, f32[24,8,128]{2,1,0:T(8,128)S(1)}, u32[]{:S(2)}, u32[]{:S(2)}) collective-permute-start(f32[24,8,128]{2,1,0:T(8,128)S(1)} %get-tuple-element.78), channel_id=1, source_target_pairs={{0,15},{1,2},{2,1},{3,4},{4,3},{5,6},{6,5},{7,8},{8,7},{9,10},{10,... | collective-permute-start | bytes 294920 | tf_op jit(solution)/shard_map/ppermute | solution.py:640
  17.9 3.0 %collective-permute-start.5 = (f32[16,8,128]{2,1,0:T(8,128)S(1)}, f32[16,8,128]{2,1,0:T(8,128)S(1)}, u32[]{:S(2)}, u32[]{:S(2)}) collective-permute-start(f32[16,8,128]{2,1,0:T(8,128)S(1)} %get-tuple-element.76), channel_id=1, source_target_pairs={{0,112},{16,32},{32,16},{48,64},{64,48},{80,96},{96,80},{112,0},{1... | collective-permute-start | bytes 196616 | tf_op jit(solution)/shard_map/ppermute | solution.py:640
  20.9 2.4 %volume.6 = (f32[1600,128]{1,0:T(8,128)S(1)}, f32[2,60,8,128]{3,2,1,0:T(8,128)S(1)}, f32[2,55,8,128]{3,2,1,0:T(8,128)S(1)}) custom-call(f32[1600,128]{1,0:T(8,128)S(1)} %get-tuple-element.68.field.refs_0_.refs_1_, f32[1600,128]{1,0:T(8,128)S(1)} %get-tuple-element.69.refs_1_, s32[10,8,128]{2,1,0:T(8,128)S(1)} %get-tuple-element.57.codes.refs_1_.refs_0_.refs_2_, ...), custom_call_target="tpu_custom_call" | custom-call | flops 10000 | bytes 10000 | tf_op jit(solution)/shard_map/volume/pallas_call | solution.py:589
  23.3 1.1 %surface.6 = (f32[1600,128]{1,0:T(8,128)S(1)}, f32[1600,128]{1,0:T(8,128)S(1)}, f32[2,55,8,128]{3,2,1,0:T(8,128)S(1)}, f32[24,8,128]{2,1,0:T(8,128)S(1)}) custom-call(s32[10,8,128]{2,1,0:T(8,128)S(1)} %get-tuple-element.57.codes.refs_1_.refs_0_.refs_2_, f32[1600,128]{1,0:T(8,128)S(1)} %get-tuple-element.68.field.refs_0_.refs_1_, ...), custom_call_target="tpu_custom_call" | custom-call | tf_op jit(solution)/shard_map/surface/pallas_call | solution.py:623
  24.4 3.1 %collective-permute-start.11 = (f32[24,8,128]{2,1,0:T(8,128)S(1)}, f32[24,8,128]{2,1,0:T(8,128)S(1)}, u32[]{:S(2)}, u32[]{:S(2)}) collective-permute-start(f32[24,8,128]{2,1,0:T(8,128)S(1)} %get-tuple-element.89), channel_id=1, source_target_pairs={{0,15},{1,2},{2,1},{3,4},{4,3},{5,6},{6,5},{7,8},{8,7},{9,10},{10,... | collective-permute-start | bytes 294920 | tf_op jit(solution)/shard_map/ppermute | solution.py:640
  27.9 2.1 %collective-permute-start.9 = (f32[16,8,128]{2,1,0:T(8,128)S(1)}, f32[16,8,128]{2,1,0:T(8,128)S(1)}, u32[]{:S(2)}, u32[]{:S(2)}) collective-permute-start(f32[16,8,128]{2,1,0:T(8,128)S(1)} %get-tuple-element.87), channel_id=1, source_target_pairs={{0,112},{16,32},{32,16},{48,64},{64,48},{80,96},{96,80},{112,0},{1... | collective-permute-start | bytes 196616 | tf_op jit(solution)/shard_map/ppermute | solution.py:640
  29.9 0.8 %collective-permute-start.8 = (f32[15,8,128]{2,1,0:T(8,128)S(1)}, f32[15,8,128]{2,1,0:T(8,128)S(1)}, u32[]{:S(2)}, u32[]{:S(2)}) collective-permute-start(f32[15,8,128]{2,1,0:T(8,128)S(1)} %get-tuple-element.86), channel_id=1, source_target_pairs={{0,16},{16,0},{32,48},{48,32},{64,80},{80,64},{96,112},{112,96},{1... | collective-permute-start | bytes 184328 | tf_op jit(solution)/shard_map/ppermute | solution.py:640
  30.7 2.4 %volume.7 = (f32[1600,128]{1,0:T(8,128)S(1)}, f32[2,60,8,128]{3,2,1,0:T(8,128)S(1)}, f32[2,55,8,128]{3,2,1,0:T(8,128)S(1)}) custom-call(f32[1600,128]{1,0:T(8,128)S(1)} %get-tuple-element.79.field.refs_0_.refs_1_, f32[1600,128]{1,0:T(8,128)S(1)} %get-tuple-element.80.refs_1_, s32[10,8,128]{2,1,0:T(8,128)S(1)} %get-tuple-element.57.codes.refs_1_.refs_0_.refs_2_, ...), custom_call_target="tpu_custom_call" | custom-call | flops 10000 | bytes 10000 | tf_op jit(solution)/shard_map/volume/pallas_call | solution.py:589
  33.1 1.1 %surface.7 = (f32[1600,128]{1,0:T(8,128)S(1)}, f32[1600,128]{1,0:T(8,128)S(1)}, f32[2,55,8,128]{3,2,1,0:T(8,128)S(1)}, f32[24,8,128]{2,1,0:T(8,128)S(1)}) custom-call(s32[10,8,128]{2,1,0:T(8,128)S(1)} %get-tuple-element.57.codes.refs_1_.refs_0_.refs_2_, f32[1600,128]{1,0:T(8,128)S(1)} %get-tuple-element.79.field.refs_0_.refs_1_, ...), custom_call_target="tpu_custom_call" | custom-call | tf_op jit(solution)/shard_map/surface/pallas_call | solution.py:623
  34.2 1.6 %collective-permute-start.15 = (f32[24,8,128]{2,1,0:T(8,128)S(1)}, f32[24,8,128]{2,1,0:T(8,128)S(1)}, u32[]{:S(2)}, u32[]{:S(2)}) collective-permute-start(f32[24,8,128]{2,1,0:T(8,128)S(1)} %get-tuple-element.100), channel_id=1, source_target_pairs={{0,15},{1,2},{2,1},{3,4},{4,3},{5,6},{6,5},{7,8},{8,7},{9,10},{10,... | collective-permute-start | bytes 294920 | tf_op jit(solution)/shard_map/ppermute | solution.py:640
  36.1 2.9 %collective-permute-start.13 = (f32[16,8,128]{2,1,0:T(8,128)S(1)}, f32[16,8,128]{2,1,0:T(8,128)S(1)}, u32[]{:S(2)}, u32[]{:S(2)}) collective-permute-start(f32[16,8,128]{2,1,0:T(8,128)S(1)} %get-tuple-element.98), channel_id=1, source_target_pairs={{0,112},{16,32},{32,16},{48,64},{64,48},{80,96},{96,80},{112,0},{1... | collective-permute-start | bytes 196616 | tf_op jit(solution)/shard_map/ppermute | solution.py:640
  39.0 2.4 %volume.8 = (f32[1600,128]{1,0:T(8,128)S(1)}, f32[2,60,8,128]{3,2,1,0:T(8,128)S(1)}, f32[2,55,8,128]{3,2,1,0:T(8,128)S(1)}) custom-call(f32[1600,128]{1,0:T(8,128)S(1)} %get-tuple-element.90.field.refs_0_.refs_1_, f32[1600,128]{1,0:T(8,128)S(1)} %get-tuple-element.91.refs_1_, s32[10,8,128]{2,1,0:T(8,128)S(1)} %get-tuple-element.57.codes.refs_1_.refs_0_.refs_2_, ...), custom_call_target="tpu_custom_call" | custom-call | flops 10000 | bytes 10000 | tf_op jit(solution)/shard_map/volume/pallas_call | solution.py:589
  41.5 1.1 %surface.8 = (f32[1600,128]{1,0:T(8,128)S(1)}, f32[1600,128]{1,0:T(8,128)S(1)}, f32[2,55,8,128]{3,2,1,0:T(8,128)S(1)}, f32[24,8,128]{2,1,0:T(8,128)S(1)}) custom-call(s32[10,8,128]{2,1,0:T(8,128)S(1)} %get-tuple-element.57.codes.refs_1_.refs_0_.refs_2_, f32[1600,128]{1,0:T(8,128)S(1)} %get-tuple-element.90.field.refs_0_.refs_1_, ...), custom_call_target="tpu_custom_call" | custom-call | tf_op jit(solution)/shard_map/surface/pallas_call | solution.py:623
  42.5 3.3 %collective-permute-start.19 = (f32[24,8,128]{2,1,0:T(8,128)S(1)}, f32[24,8,128]{2,1,0:T(8,128)S(1)}, u32[]{:S(2)}, u32[]{:S(2)}) collective-permute-start(f32[24,8,128]{2,1,0:T(8,128)S(1)} %get-tuple-element.111), channel_id=1, source_target_pairs={{0,15},{1,2},{2,1},{3,4},{4,3},{5,6},{6,5},{7,8},{8,7},{9,10},{10,... | collective-permute-start | bytes 294920 | tf_op jit(solution)/shard_map/ppermute | solution.py:640
  46.2 1.9 %collective-permute-start.17 = (f32[16,8,128]{2,1,0:T(8,128)S(1)}, f32[16,8,128]{2,1,0:T(8,128)S(1)}, u32[]{:S(2)}, u32[]{:S(2)}) collective-permute-start(f32[16,8,128]{2,1,0:T(8,128)S(1)} %get-tuple-element.109), channel_id=1, source_target_pairs={{0,112},{16,32},{32,16},{48,64},{64,48},{80,96},{96,80},{112,0},{1... | collective-permute-start | bytes 196616 | tf_op jit(solution)/shard_map/ppermute | solution.py:640
  48.1 1.0 %collective-permute-start.16 = (f32[15,8,128]{2,1,0:T(8,128)S(1)}, f32[15,8,128]{2,1,0:T(8,128)S(1)}, u32[]{:S(2)}, u32[]{:S(2)}) collective-permute-start(f32[15,8,128]{2,1,0:T(8,128)S(1)} %get-tuple-element.108), channel_id=1, source_target_pairs={{0,16},{16,0},{32,48},{48,32},{64,80},{80,64},{96,112},{112,96},{1... | collective-permute-start | bytes 184328 | tf_op jit(solution)/shard_map/ppermute | solution.py:640
  49.1 2.4 %volume.9 = (f32[1600,128]{1,0:T(8,128)S(1)}, f32[2,60,8,128]{3,2,1,0:T(8,128)S(1)}, f32[2,55,8,128]{3,2,1,0:T(8,128)S(1)}) custom-call(f32[1600,128]{1,0:T(8,128)S(1)} %get-tuple-element.101.field.refs_0_.refs_1_, f32[1600,128]{1,0:T(8,128)S(1)} %get-tuple-element.102.refs_1_, s32[10,8,128]{2,1,0:T(8,128)S(1)} %get-tuple-element.57.codes.refs_1_.refs_0_.refs_2_, ...), custom_call_target="tpu_custom_call" | custom-call | flops 10000 | bytes 10000 | tf_op jit(solution)/shard_map/volume/pallas_call | solution.py:589
  51.5 1.7 %surface.9 = (f32[5,6,6,6,128]{4,3,2,1,0:T(8,128)}, f32[5,6,6,6,128]{4,3,2,1,0:T(8,128)}) custom-call(s32[10,8,128]{2,1,0:T(8,128)S(1)} %get-tuple-element.57.codes.refs_1_.refs_0_.refs_2_, f32[1600,128]{1,0:T(8,128)S(1)} %get-tuple-element.101.field.refs_0_.refs_1_, f32[1600,128]{1,0:T(8,128)S(1)} %get-tuple-element.105.refs_2_, ...), custom_call_target="tpu_custom_call" | custom-call | tf_op jit(solution)/shard_map/surface/pallas_call | solution.py:623
  (32 shorter events, 2.2 us)
Async XLA Ops:
  2.1 12.8 %collective-permute-start.3 = (f32[24,8,128]{2,1,0:T(8,128)S(1)}, f32[24,8,128]{2,1,0:T(8,128)S(1)}, u32[]{:S(2)}, u32[]{:S(2)}) collective-permute-start(f32[24,8,128]{2,1,0:T(8,128)S(1)} %get-tuple-element.67), channel_id=1, source_target_pairs={{0,15},{1,2},{2,1},{3,4},{4,3},{5,6},{6,5},{7,8},{8,7},{9,10},{10,... | collective-permute-start | bytes 294920 | tf_op jit(solution)/shard_map/ppermute | solution.py:640
  9.5 5.4 %collective-permute-start.2 = (f32[23,8,128]{2,1,0:T(8,128)S(1)}, f32[23,8,128]{2,1,0:T(8,128)S(1)}, u32[]{:S(2)}, u32[]{:S(2)}) collective-permute-start(f32[23,8,128]{2,1,0:T(8,128)S(1)} %get-tuple-element.66), channel_id=1, source_target_pairs={{0,1},{1,0},{2,3},{3,2},{4,5},{5,4},{6,7},{7,6},{8,9},{9,8},{10,11... | collective-permute-start | bytes 282632 | tf_op jit(solution)/shard_map/ppermute | solution.py:640
  9.6 5.3 %collective-permute-start.1 = (f32[16,8,128]{2,1,0:T(8,128)S(1)}, f32[16,8,128]{2,1,0:T(8,128)S(1)}, u32[]{:S(2)}, u32[]{:S(2)}) collective-permute-start(f32[16,8,128]{2,1,0:T(8,128)S(1)} %get-tuple-element.65), channel_id=1, source_target_pairs={{0,112},{16,32},{32,16},{48,64},{64,48},{80,96},{96,80},{112,0},{1... | collective-permute-start | bytes 196616 | tf_op jit(solution)/shard_map/ppermute | solution.py:640
  11.8 3.2 %collective-permute-start = (f32[15,8,128]{2,1,0:T(8,128)S(1)}, f32[15,8,128]{2,1,0:T(8,128)S(1)}, u32[]{:S(2)}, u32[]{:S(2)}) collective-permute-start(f32[15,8,128]{2,1,0:T(8,128)S(1)} %get-tuple-element.64), channel_id=1, source_target_pairs={{0,16},{16,0},{32,48},{48,32},{64,80},{80,64},{96,112},{112,96},{1... | collective-permute-start | bytes 184328 | tf_op jit(solution)/shard_map/ppermute | solution.py:640
  16.1 7.2 %collective-permute-start.7 = (f32[24,8,128]{2,1,0:T(8,128)S(1)}, f32[24,8,128]{2,1,0:T(8,128)S(1)}, u32[]{:S(2)}, u32[]{:S(2)}) collective-permute-start(f32[24,8,128]{2,1,0:T(8,128)S(1)} %get-tuple-element.78), channel_id=1, source_target_pairs={{0,15},{1,2},{2,1},{3,4},{4,3},{5,6},{6,5},{7,8},{8,7},{9,10},{10,... | collective-permute-start | bytes 294920 | tf_op jit(solution)/shard_map/ppermute | solution.py:640
  17.5 5.8 %collective-permute-start.6 = (f32[23,8,128]{2,1,0:T(8,128)S(1)}, f32[23,8,128]{2,1,0:T(8,128)S(1)}, u32[]{:S(2)}, u32[]{:S(2)}) collective-permute-start(f32[23,8,128]{2,1,0:T(8,128)S(1)} %get-tuple-element.77), channel_id=1, source_target_pairs={{0,1},{1,0},{2,3},{3,2},{4,5},{5,4},{6,7},{7,6},{8,9},{9,8},{10,11... | collective-permute-start | bytes 282632 | tf_op jit(solution)/shard_map/ppermute | solution.py:640
  17.9 5.4 %collective-permute-start.5 = (f32[16,8,128]{2,1,0:T(8,128)S(1)}, f32[16,8,128]{2,1,0:T(8,128)S(1)}, u32[]{:S(2)}, u32[]{:S(2)}) collective-permute-start(f32[16,8,128]{2,1,0:T(8,128)S(1)} %get-tuple-element.76), channel_id=1, source_target_pairs={{0,112},{16,32},{32,16},{48,64},{64,48},{80,96},{96,80},{112,0},{1... | collective-permute-start | bytes 196616 | tf_op jit(solution)/shard_map/ppermute | solution.py:640
  20.8 2.4 %collective-permute-start.4 = (f32[15,8,128]{2,1,0:T(8,128)S(1)}, f32[15,8,128]{2,1,0:T(8,128)S(1)}, u32[]{:S(2)}, u32[]{:S(2)}) collective-permute-start(f32[15,8,128]{2,1,0:T(8,128)S(1)} %get-tuple-element.75), channel_id=1, source_target_pairs={{0,16},{16,0},{32,48},{48,32},{64,80},{80,64},{96,112},{112,96},{1... | collective-permute-start | bytes 184328 | tf_op jit(solution)/shard_map/ppermute | solution.py:640
  24.4 8.7 %collective-permute-start.11 = (f32[24,8,128]{2,1,0:T(8,128)S(1)}, f32[24,8,128]{2,1,0:T(8,128)S(1)}, u32[]{:S(2)}, u32[]{:S(2)}) collective-permute-start(f32[24,8,128]{2,1,0:T(8,128)S(1)} %get-tuple-element.89), channel_id=1, source_target_pairs={{0,15},{1,2},{2,1},{3,4},{4,3},{5,6},{6,5},{7,8},{8,7},{9,10},{10,... | collective-permute-start | bytes 294920 | tf_op jit(solution)/shard_map/ppermute | solution.py:640
  27.8 5.4 %collective-permute-start.10 = (f32[23,8,128]{2,1,0:T(8,128)S(1)}, f32[23,8,128]{2,1,0:T(8,128)S(1)}, u32[]{:S(2)}, u32[]{:S(2)}) collective-permute-start(f32[23,8,128]{2,1,0:T(8,128)S(1)} %get-tuple-element.88), channel_id=1, source_target_pairs={{0,1},{1,0},{2,3},{3,2},{4,5},{5,4},{6,7},{7,6},{8,9},{9,8},{10,11... | collective-permute-start | bytes 282632 | tf_op jit(solution)/shard_map/ppermute | solution.py:640
  27.9 5.3 %collective-permute-start.9 = (f32[16,8,128]{2,1,0:T(8,128)S(1)}, f32[16,8,128]{2,1,0:T(8,128)S(1)}, u32[]{:S(2)}, u32[]{:S(2)}) collective-permute-start(f32[16,8,128]{2,1,0:T(8,128)S(1)} %get-tuple-element.87), channel_id=1, source_target_pairs={{0,112},{16,32},{32,16},{48,64},{64,48},{80,96},{96,80},{112,0},{1... | collective-permute-start | bytes 196616 | tf_op jit(solution)/shard_map/ppermute | solution.py:640
  29.9 3.2 %collective-permute-start.8 = (f32[15,8,128]{2,1,0:T(8,128)S(1)}, f32[15,8,128]{2,1,0:T(8,128)S(1)}, u32[]{:S(2)}, u32[]{:S(2)}) collective-permute-start(f32[15,8,128]{2,1,0:T(8,128)S(1)} %get-tuple-element.86), channel_id=1, source_target_pairs={{0,16},{16,0},{32,48},{48,32},{64,80},{80,64},{96,112},{112,96},{1... | collective-permute-start | bytes 184328 | tf_op jit(solution)/shard_map/ppermute | solution.py:640
  34.2 7.2 %collective-permute-start.15 = (f32[24,8,128]{2,1,0:T(8,128)S(1)}, f32[24,8,128]{2,1,0:T(8,128)S(1)}, u32[]{:S(2)}, u32[]{:S(2)}) collective-permute-start(f32[24,8,128]{2,1,0:T(8,128)S(1)} %get-tuple-element.100), channel_id=1, source_target_pairs={{0,15},{1,2},{2,1},{3,4},{4,3},{5,6},{6,5},{7,8},{8,7},{9,10},{10,... | collective-permute-start | bytes 294920 | tf_op jit(solution)/shard_map/ppermute | solution.py:640
  36.1 5.4 %collective-permute-start.14 = (f32[23,8,128]{2,1,0:T(8,128)S(1)}, f32[23,8,128]{2,1,0:T(8,128)S(1)}, u32[]{:S(2)}, u32[]{:S(2)}) collective-permute-start(f32[23,8,128]{2,1,0:T(8,128)S(1)} %get-tuple-element.99), channel_id=1, source_target_pairs={{0,1},{1,0},{2,3},{3,2},{4,5},{5,4},{6,7},{7,6},{8,9},{9,8},{10,11... | collective-permute-start | bytes 282632 | tf_op jit(solution)/shard_map/ppermute | solution.py:640
  36.1 5.3 %collective-permute-start.13 = (f32[16,8,128]{2,1,0:T(8,128)S(1)}, f32[16,8,128]{2,1,0:T(8,128)S(1)}, u32[]{:S(2)}, u32[]{:S(2)}) collective-permute-start(f32[16,8,128]{2,1,0:T(8,128)S(1)} %get-tuple-element.98), channel_id=1, source_target_pairs={{0,112},{16,32},{32,16},{48,64},{64,48},{80,96},{96,80},{112,0},{1... | collective-permute-start | bytes 196616 | tf_op jit(solution)/shard_map/ppermute | solution.py:640
  39.0 2.4 %collective-permute-start.12 = (f32[15,8,128]{2,1,0:T(8,128)S(1)}, f32[15,8,128]{2,1,0:T(8,128)S(1)}, u32[]{:S(2)}, u32[]{:S(2)}) collective-permute-start(f32[15,8,128]{2,1,0:T(8,128)S(1)} %get-tuple-element.97), channel_id=1, source_target_pairs={{0,16},{16,0},{32,48},{48,32},{64,80},{80,64},{96,112},{112,96},{1... | collective-permute-start | bytes 184328 | tf_op jit(solution)/shard_map/ppermute | solution.py:640
  42.5 9.0 %collective-permute-start.19 = (f32[24,8,128]{2,1,0:T(8,128)S(1)}, f32[24,8,128]{2,1,0:T(8,128)S(1)}, u32[]{:S(2)}, u32[]{:S(2)}) collective-permute-start(f32[24,8,128]{2,1,0:T(8,128)S(1)} %get-tuple-element.111), channel_id=1, source_target_pairs={{0,15},{1,2},{2,1},{3,4},{4,3},{5,6},{6,5},{7,8},{8,7},{9,10},{10,... | collective-permute-start | bytes 294920 | tf_op jit(solution)/shard_map/ppermute | solution.py:640
  46.1 5.4 %collective-permute-start.18 = (f32[23,8,128]{2,1,0:T(8,128)S(1)}, f32[23,8,128]{2,1,0:T(8,128)S(1)}, u32[]{:S(2)}, u32[]{:S(2)}) collective-permute-start(f32[23,8,128]{2,1,0:T(8,128)S(1)} %get-tuple-element.110), channel_id=1, source_target_pairs={{0,1},{1,0},{2,3},{3,2},{4,5},{5,4},{6,7},{7,6},{8,9},{9,8},{10,11... | collective-permute-start | bytes 282632 | tf_op jit(solution)/shard_map/ppermute | solution.py:640
  46.2 5.3 %collective-permute-start.17 = (f32[16,8,128]{2,1,0:T(8,128)S(1)}, f32[16,8,128]{2,1,0:T(8,128)S(1)}, u32[]{:S(2)}, u32[]{:S(2)}) collective-permute-start(f32[16,8,128]{2,1,0:T(8,128)S(1)} %get-tuple-element.109), channel_id=1, source_target_pairs={{0,112},{16,32},{32,16},{48,64},{64,48},{80,96},{96,80},{112,0},{1... | collective-permute-start | bytes 196616 | tf_op jit(solution)/shard_map/ppermute | solution.py:640
  48.1 3.4 %collective-permute-start.16 = (f32[15,8,128]{2,1,0:T(8,128)S(1)}, f32[15,8,128]{2,1,0:T(8,128)S(1)}, u32[]{:S(2)}, u32[]{:S(2)}) collective-permute-start(f32[15,8,128]{2,1,0:T(8,128)S(1)} %get-tuple-element.108), channel_id=1, source_target_pairs={{0,16},{16,0},{32,48},{48,32},{64,80},{80,64},{96,112},{112,96},{1... | collective-permute-start | bytes 184328 | tf_op jit(solution)/shard_map/ppermute | solution.py:640
